TPU v7x, 128 devices: a whole 4x4x4 slice. The times are simulated.
128 devices in a mesh: gx: 8 (over z_lo, y), gy: 16 (over z_hi, x, core).
Axes of the slice: x: 4, y: 4, z: 4 (z_hi: 2, z_lo: 2; z = z_hi * 2 + z_lo), core: 2. Of those that a mesh axis runs over, the one named last changes fastest.
Arguments:
- thermal_rows: float32 [196608, 128], P(('gx', 'gy')), may hold values from -6 to 6
- row_owner: int32 [196608, 1], P(('gx', 'gy')), may hold values from 0 to 127; in each aligned block of 1536 rows (0 to 1535, 1536 to 3071, ...) at most 24 rows name the same one
- row_element: int32 [196608, 1], P(('gx', 'gy')), may hold values from 0 to 1023
- modulus: float32 [64, 128, 2048], P(None, 'gx', 'gy'), may hold values from 0.5 to 5
- birth: int32 [64, 128, 2048], P(None, 'gx', 'gy'), may hold values from 0 to 4
- start_disp: float32 [3, 64, 128, 2048], P(None, None, 'gx', 'gy'), may hold values from -6 to 6
- bounds: float32 [2], replicated, as said below
Outputs:
- displacement: float32 [3, 64, 128, 2048], P(None, None, 'gx', 'gy')
Inputs may be any that keep to these rules, and one draw needn't show every extreme that they name: `row_owner`: no device holds more than 24 rows for one tile, and some device holds exactly 24 rows for some tile. `bounds`: 0 < lo < hi.
All inputs are finite; a program needn't handle non-finite values.
Results may differ from a plain program's by a relative error of at most 0.00002.
Values sent between devices are 32-bit elements; how exact they have to be, the bound alone decides.
A program may use at most 192 MiB of HBM per device.

v0:
```python
import jax
import jax.numpy as jnp
from jax import lax
from jax.sharding import PartitionSpec as P

SWEEPS = 4
CAP = 24


NEIGHBOUR_WEIGHTS = (0.0, 1.0, 0.5, 0.25)
DIAGONAL_WEIGHT = 14.5
COUPLING = 0.25
SOFTENED = 0.05


def with_halo(cells, sides, width):
    for axis, dim in sides:
        count = lax.axis_size(axis)
        ends = count - 1
        head = lax.slice_in_dim(cells, 0, width, axis=dim)
        tail = lax.slice_in_dim(cells, cells.shape[dim] - width, cells.shape[dim], axis=dim)
        cells = jnp.concatenate(
            [
                lax.ppermute(tail, axis, [(i, (i + 1) % count) for i in range(ends)]),
                cells,
                lax.ppermute(head, axis, [((i + 1) % count, i) for i in range(ends)]),
            ],
            axis=dim,
        )
    return cells


def operate(padded, modulus_now):
    depth = padded.shape[1] - 2
    breadth = padded.shape[2] - 2
    length = padded.shape[3] - 2

    def neighbour(a, b, c):
        return padded[:, 1 + a : 1 + a + depth, 1 + b : 1 + b + breadth, 1 + c : 1 + c + length]

    middle = neighbour(0, 0, 0)
    beside_all = jnp.zeros_like(middle)
    for a in (-1, 0, 1):
        for b in (-1, 0, 1):
            for c in (-1, 0, 1):
                distance = abs(a) + abs(b) + abs(c)
                if distance:
                    beside_all = beside_all + NEIGHBOUR_WEIGHTS[distance] * neighbour(a, b, c)
    unit_steps = ((1, 0, 0), (0, 1, 0), (0, 0, 1))
    coupled = []
    for component in range(3):
        summed = jnp.zeros_like(middle[0])
        for second in range(3):
            if second != component:
                e = unit_steps[component]
                f = unit_steps[second]
                plus_plus = neighbour(e[0] + f[0], e[1] + f[1], e[2] + f[2])[second]
                plus_minus = neighbour(e[0] - f[0], e[1] - f[1], e[2] - f[2])[second]
                minus_plus = neighbour(f[0] - e[0], f[1] - e[1], f[2] - e[2])[second]
                minus_minus = neighbour(-e[0] - f[0], -e[1] - f[1], -e[2] - f[2])[second]
                summed = summed + 0.25 * (plus_plus - plus_minus - minus_plus + minus_minus)
        coupled.append(summed)
    return modulus_now * (DIAGONAL_WEIGHT * middle - beside_all - COUPLING * jnp.stack(coupled))


def load_from(padded_stress):
    along_z = 0.5 * (padded_stress[2:, 1:-1, 1:-1] - padded_stress[:-2, 1:-1, 1:-1])
    along_x = 0.5 * (padded_stress[1:-1, 2:, 1:-1] - padded_stress[1:-1, :-2, 1:-1])
    along_y = 0.5 * (padded_stress[1:-1, 1:-1, 2:] - padded_stress[1:-1, 1:-1, :-2])
    return jnp.stack([along_z, along_x, along_y])


def padded_field(field):
    extended = with_halo(field, (("gx", 2), ("gy", 3)), 1)
    return jnp.pad(extended, ((0, 0), (1, 1), (0, 0), (0, 0)))


def advance(step_prev, scaled, sweep, ratio_now, sigma, delta, theta):
    if sweep == 0:
        return (scaled / theta, ratio_now)
    ratio_next = 1.0 / (2.0 * sigma - ratio_now)
    return (ratio_next * ratio_now * step_prev + 2.0 * ratio_next / delta * scaled, ratio_next)


def local(thermal_rows, row_owner, row_element, modulus, birth, start_disp, bounds):
    tiles_x = lax.axis_size("gx")
    tiles_y = lax.axis_size("gy")
    tiles = tiles_x * tiles_y
    depth = modulus.shape[0]
    breadth = modulus.shape[1]
    length = modulus.shape[2]
    elements = depth * breadth
    owner = row_owner[:, 0]
    onehot = (owner[:, None] == jnp.arange(tiles, dtype=jnp.int32)[None, :]).astype(jnp.int32)
    before = jnp.cumsum(onehot, axis=0) - onehot
    slot = jnp.sum(before * onehot, axis=1)
    position = owner * CAP + slot
    send_rows = jnp.zeros((tiles * CAP, length), jnp.float32).at[position].set(thermal_rows)
    send_ids = jnp.full((tiles * CAP,), elements, jnp.int32).at[position].set(row_element[:, 0])
    got_rows, got_ids = (
        lax.all_to_all(send_rows, ("gx", "gy"), split_axis=0, concat_axis=0, tiled=True),
        lax.all_to_all(send_ids, ("gx", "gy"), split_axis=0, concat_axis=0, tiled=True),
    )
    summed_rows = jax.ops.segment_sum(got_rows, got_ids, num_segments=elements + 1)
    increment = summed_rows[:elements].reshape(depth, breadth, length)
    stress = modulus * increment
    lower = bounds[0]
    upper = bounds[1]
    theta = (upper + lower) / 2.0
    delta = (upper - lower) / 2.0
    sigma = theta / delta
    ratio_now = 1.0 / sigma
    field = start_disp
    step_field = jnp.zeros_like(field)
    stress_ext = with_halo(stress, (("gx", 1), ("gy", 2)), 1)
    load = load_from(jnp.pad(stress_ext, ((1, 1), (0, 0), (0, 0))))
    first_padded = padded_field(field)
    for sweep in range(SWEEPS):
        active = modulus * jnp.where(birth <= sweep, 1.0, SOFTENED).astype(jnp.float32)
        if sweep == 0:
            padded = first_padded
        else:
            padded = padded_field(field)
        residual = load - operate(padded, active)
        scaled = residual / (DIAGONAL_WEIGHT * active)
        step_field, ratio_now = advance(step_field, scaled, sweep, ratio_now, sigma, delta, theta)
        field = field + step_field
    return field


def solution(mesh):
    placed = (
        P(("gx", "gy"), None),
        P(("gx", "gy"), None),
        P(("gx", "gy"), None),
        P(None, "gx", "gy"),
        P(None, "gx", "gy"),
        P(None, None, "gx", "gy"),
        P(),
    )
    return jax.shard_map(
        local, mesh=mesh, in_specs=placed, out_specs=P(None, None, "gx", "gy"), check_vma=False
    )
```

profile of v0, /device:TPU:31, one launch (start us, length us, event | category | flops | bytes accessed | tf_op | source)
XLA Modules:
  0.0 352.3 jit_solution(12405453713037606681)
XLA Ops:
  9.0 6.2 %scatter_custom_fusion = s32[3072]{0:T(1024)S(1)} fusion(s32[1536]{0:T(1024)S(1)} %fusion.147, s32[1536]{0:T(1024)S(1)} %reduce.3, s32[]{:T(128)} %constant.17.clone.1), kind=kCustom, calls=%fused_computation.395 | custom fusion | bytes 12292 | tf_op jit(solution)/shard_map/scatter | solution.py:99
  15.9 11.1 %all-to-all-start = ((s32[128,24,1]{1,2,0:T(1,128)}), s32[128,24,1]{1,2,0:T(1,128)S(1)}, u32[]{:S(2)}, u32[]{:S(2)}) async-start(s32[128,24,1]{1,2,0:T(1,128)} %bitcast.3), calls=%async_computation | async-start | bytes 131072 | tf_op jit(solution)/shard_map/all_to_all | solution.py:102
  27.0 5.9 %scatter_custom_fusion.1 = f32[3072,128]{1,0:T(8,128)} fusion(s32[1536]{0:T(1024)S(1)} %fusion.147, f32[1536,128]{1,0:T(8,128)} %param.7, f32[]{:T(128)} %constant.16.clone.1), kind=kCustom, calls=%fused_computation.264 | custom fusion | bytes 1573376 | tf_op jit(solution)/shard_map/scatter | solution.py:98
  34.7 9.8 %all-to-all-start.1 = ((f32[128,24,128]{2,1,0:T(8,128)}), f32[128,24,128]{2,1,0:T(8,128)S(1)}, u32[]{:S(2)}, u32[]{:S(2)}) async-start(f32[128,24,128]{2,1,0:T(8,128)} %bitcast.4), calls=%async_computation.1 | async-start | bytes 3145728 | tf_op jit(solution)/shard_map/all_to_all | solution.py:101
  44.5 5.2 %fusion.157 = (f32[3,64,18,1]{3,2,1,0:T(8,128)}, f32[3,64,18,1]{3,2,1,0:T(8,128)}) fusion(f32[3,64,18,128]{3,2,1,0:T(8,128)} %pad_maximum_fusion.4), kind=kLoop, calls=%fused_computation.403 | loop fusion | bytes 55296 | tf_op jit(solution)/shard_map/slice | solution.py:20
  52.2 5.5 %collective-permute-start.6 = (f32[3,64,18,1]{1,2,3,0:T(8,128)S(1)}, f32[3,64,18,1]{1,2,3,0:T(8,128)}, u32[]{:S(2)}, u32[]{:S(2)}) collective-permute-start(f32[3,64,18,1]{1,2,3,0:T(8,128)S(1)} %copy.90), channel_id=1, source_target_pairs={{0,1},{1,2},{2,3},{3,4},{4,5},{5,6},{6,7},{7,8},{8,9},{9,10},{10,1... | collective-permute-start | bytes 41480 | tf_op jit(solution)/shard_map/ppermute | solution.py:24
  72.8 5.7 %select_maximum_fusion.12 = f32[3,66,18,130]{3,2,1,0:T(8,128)S(1)} fusion(f32[3,64,18,1]{3,2,1,0:T(8,128)} %copy.93, f32[3,64,18,1]{3,2,1,0:T(8,128)} %copy.92, f32[3,64,1,128]{3,2,1,0:T(1,128)S(1)} %bitcast.63, f32[3,64,16,128]{3,2,1,0:T(8,128)S(1)} %copy-done.2, f32[3,64,1,128]{3,2,1,0:T(1,128)S(1)} %bitcast.57), kind=kLoop, calls=%fused_computation.17 | loop fusion | flops 5559840 | bytes 3650400 | tf_op jit(solution)/shard_map/concatenate | solution.py:22
  81.2 5.3 %maximum_maximum_fusion = (f32[3,64,18,129]{3,2,1,0:T(8,128)}, f32[3,64,18,129]{3,2,1,0:T(8,128)}) fusion(f32[3,64,1,128]{3,2,1,0:T(1,128)S(1)} %bitcast.65, f32[3,64,16,128]{3,2,1,0:T(8,128)S(1)} %copy-done.2, f32[3,64,1,128]{3,2,1,0:T(1,128)S(1)} %bitcast.59, f32[3,64,18,1]{3,2,1,0:T(8,128)S(1)} %copy-done.3, f32[3,64,18,1]{3,2,1,0:T(8,128)S(1)} %copy-done.5), kind=kLoop, calls=%fused_computation.22 | loop fusion | flops 2674944 | bytes 5363712 | tf_op jit(solution)/shard_map/concatenate | solution.py:22
  87.7 17.4 %scatter_custom_fusion.2 = f32[1025,128]{1,0:T(8,128)S(1)} fusion(s32[3072]{0:T(1024)S(1)} %reshape.64, f32[3072,128]{1,0:T(8,128)} %bitcast.93, f32[]{:T(128)} %constant.16.clone.1), kind=kCustom, calls=%fused_computation.386 | custom fusion | flops 393216 | bytes 525312 | tf_op jit(solution)/shard_map/scatter-add | solution.py:104
  113.8 5.0 %fusion.131 = f32[1,64,16,128]{3,2,1,0:T(8,128)} fusion(f32[3,64,18,1]{3,2,1,0:T(8,128)S(1)} %copy-done.4, f32[3,64,1,128]{3,2,1,0:T(1,128)S(1)} %bitcast.66, f32[3,64,16,128]{3,2,1,0:T(8,128)S(1)} %copy-done.2, f32[3,64,1,128]{3,2,1,0:T(1,128)S(1)} %bitcast.60, f32[3,64,18,1]{3,2,1,0:T(8,128)S(1)} %copy-done.6, f32[3,66,18,130]{3,2,1,0:T(8,128)} %copy-done), kind=kLoop, calls=%fused_computation.341 | loop fusion | flops 2621440 | bytes 4418560 | tf_op jit(solution)/shard_map/add | solution.py:61
  119.5 8.5 %collective-permute-start.2 = (f32[64,18,1]{0,2,1:T(1,128)S(1)}, f32[64,18,1]{0,2,1:T(1,128)S(1)}, u32[]{:S(2)}, u32[]{:S(2)}) collective-permute-start(f32[64,18,1]{0,2,1:T(1,128)S(1)} %copy.80), channel_id=1, source_target_pairs={{0,1},{1,2},{2,3},{3,4},{4,5},{5,6},{6,7},{7,8},{8,9},{9,10},{10,1... | collective-permute-start | bytes 13832 | tf_op jit(solution)/shard_map/ppermute | solution.py:24
  130.3 6.3 %fusion.135 = f32[1,64,16,128]{3,2,1,0:T(8,128)} fusion(f32[3,66,18,130]{3,2,1,0:T(8,128)} %copy-done), kind=kLoop, calls=%fused_computation.357 | loop fusion | flops 1048576 | bytes 4718592 | tf_op jit(solution)/shard_map/add | solution.py:61
  141.7 12.9 %fusion.152 = (f32[3,64,16,128]{3,2,1,0:T(8,128)S(1)}, f32[3,64,16,128]{3,2,1,0:T(8,128)}) fusion(f32[3,64,16,128]{3,2,1,0:T(8,128)} %param.12, f32[64,16,128]{2,1,0:T(8,128)} %get-tuple-element.45, f32[1,64,16,128]{3,2,1,0:T(8,128)} %fusion.131, f32[1,64,16,128]{3,2,1,0:T(8,128)} %fusion.133, f32[1,64,16,128]{3,2,1,0:T(8,128)} %fusion.135, ...), kind=kLoop, calls=%fused_computation.399 | loop fusion | flops 23199744 | bytes 46858240 | tf_op jit(solution)/shard_map/add | solution.py:127
  160.9 5.5 %collective-permute-done.9 = f32[3,64,1,128]{3,1,2,0:T(8,128)S(1)} collective-permute-done((f32[3,64,1,128]{3,1,2,0:T(8,128)S(1)}, f32[3,64,1,128]{3,1,2,0:T(8,128)S(1)}, u32[]{:S(2)}, u32[]{:S(2)}) %collective-permute-start.9) | collective-permute-done | bytes 98336 | tf_op jit(solution)/shard_map/ppermute | solution.py:26
  172.1 9.3 %collective-permute-start.10 = (f32[3,64,18,1]{1,2,3,0:T(8,128)S(1)}, f32[3,64,18,1]{1,2,3,0:T(8,128)S(1)}, u32[]{:S(2)}, u32[]{:S(2)}) collective-permute-start(f32[3,64,18,1]{1,2,3,0:T(8,128)S(1)} %copy.102), channel_id=1, source_target_pairs={{0,1},{1,2},{2,3},{3,4},{4,5},{5,6},{6,7},{7,8},{8,9},{9,10},{10,1... | collective-permute-start | bytes 41480 | tf_op jit(solution)/shard_map/ppermute | solution.py:24
  194.9 7.1 %maximum_maximum_fusion.1 = (f32[3,64,18,129]{3,2,1,0:T(8,128)}, f32[3,64,18,129]{3,2,1,0:T(8,128)}) fusion(f32[3,64,1,128]{3,2,1,0:T(1,128)S(1)} %bitcast.75, f32[3,64,16,128]{3,2,1,0:T(8,128)S(1)} %get-tuple-element.15, f32[3,64,1,128]{3,2,1,0:T(1,128)S(1)} %bitcast.69, f32[3,64,18,1]{3,2,1,0:T(8,128)} %copy.104, f32[3,64,18,1]{3,2,1,0:T(8,128)} %copy.105), kind=kLoop, calls=%fused_computation.24 | loop fusion | flops 2674944 | bytes 5363712 | tf_op jit(solution)/shard_map/concatenate | solution.py:22
  212.7 12.4 %fusion.151 = (f32[3,64,16,128]{3,2,1,0:T(8,128)}, f32[3,64,16,128]{3,2,1,0:T(8,128)}) fusion(f32[3,64,16,128]{3,2,1,0:T(8,128)S(1)} %get-tuple-element.15, f32[64,16,128]{2,1,0:T(8,128)} %get-tuple-element.43, f32[1,64,16,128]{3,2,1,0:T(8,128)} %fusion.125, f32[1,64,16,128]{3,2,1,0:T(8,128)} %fusion.127, f32[1,64,16,128]{3,2,1,0:T(8,128)} %fusion.129, ...), kind=kLoop, calls=%fused_computation.398 | loop fusion | flops 24379392 | bytes 48431112 | tf_op jit(solution)/shard_map/add | solution.py:127
  242.4 5.3 %collective-permute-start.14 = (f32[3,64,18,1]{1,2,3,0:T(8,128)S(1)}, f32[3,64,18,1]{1,2,3,0:T(8,128)S(1)}, u32[]{:S(2)}, u32[]{:S(2)}) collective-permute-start(f32[3,64,18,1]{1,2,3,0:T(8,128)S(1)} %copy.114), channel_id=1, source_target_pairs={{0,1},{1,2},{2,3},{3,4},{4,5},{5,6},{6,7},{7,8},{8,9},{9,10},{10,1... | collective-permute-start | bytes 41480 | tf_op jit(solution)/shard_map/ppermute | solution.py:24
  252.7 4.7 %collective-permute-done.15 = f32[3,64,18,1]{1,2,3,0:T(8,128)S(1)} collective-permute-done((f32[3,64,18,1]{1,2,3,0:T(8,128)S(1)}, f32[3,64,18,1]{1,2,3,0:T(8,128)S(1)}, u32[]{:S(2)}, u32[]{:S(2)}) %collective-permute-start.15) | collective-permute-done | bytes 13856 | tf_op jit(solution)/shard_map/ppermute | solution.py:26
  259.6 7.1 %maximum_maximum_fusion.2 = (f32[3,64,18,129]{3,2,1,0:T(8,128)}, f32[3,64,18,129]{3,2,1,0:T(8,128)}) fusion(f32[3,64,1,128]{3,2,1,0:T(1,128)S(1)} %bitcast.87, f32[3,64,16,128]{3,2,1,0:T(8,128)S(1)} %copy-done.1, f32[3,64,1,128]{3,2,1,0:T(1,128)S(1)} %bitcast.81, f32[3,64,18,1]{3,2,1,0:T(8,128)} %copy.116, f32[3,64,18,1]{3,2,1,0:T(8,128)} %copy.117), kind=kLoop, calls=%fused_computation.26 | loop fusion | flops 2674944 | bytes 5363712 | tf_op jit(solution)/shard_map/concatenate | solution.py:22
  277.3 12.5 %fusion.150 = (f32[3,64,16,128]{3,2,1,0:T(8,128)S(1)}, f32[3,64,16,128]{3,2,1,0:T(8,128)}) fusion(f32[3,64,16,128]{3,2,1,0:T(8,128)S(1)} %copy-done.1, f32[64,16,128]{2,1,0:T(8,128)} %get-tuple-element.47, f32[1,64,16,128]{3,2,1,0:T(8,128)} %fusion.119, f32[1,64,16,128]{3,2,1,0:T(8,128)} %fusion.121, f32[1,64,16,128]{3,2,1,0:T(8,128)} %fusion.123, ...), kind=kLoop, calls=%fused_computation.397 | loop fusion | flops 24379392 | bytes 48431112 | tf_op jit(solution)/shard_map/add | solution.py:127
  315.4 4.7 %collective-permute-done.19 = f32[3,64,18,1]{1,2,3,0:T(8,128)S(1)} collective-permute-done((f32[3,64,18,1]{1,2,3,0:T(8,128)S(1)}, f32[3,64,18,1]{1,2,3,0:T(8,128)S(1)}, u32[]{:S(2)}, u32[]{:S(2)}) %collective-permute-start.19) | collective-permute-done | bytes 13856 | tf_op jit(solution)/shard_map/ppermute | solution.py:26
  322.3 7.1 %maximum_maximum_fusion.3 = (f32[3,64,18,129]{3,2,1,0:T(8,128)}, f32[3,64,18,129]{3,2,1,0:T(8,128)}) fusion(f32[3,64,1,128]{3,2,1,0:T(1,128)S(1)} %bitcast.51, f32[3,64,16,128]{3,2,1,0:T(8,128)S(1)} %get-tuple-element.7, f32[3,64,1,128]{3,2,1,0:T(1,128)S(1)} %bitcast.45, f32[3,64,18,1]{3,2,1,0:T(8,128)} %copy.128, f32[3,64,18,1]{3,2,1,0:T(8,128)} %copy.129), kind=kLoop, calls=%fused_computation.28 | loop fusion | flops 2674944 | bytes 5363712 | tf_op jit(solution)/shard_map/concatenate | solution.py:22
  340.1 12.1 %add_add_fusion = f32[3,64,16,128]{3,2,1,0:T(8,128)} fusion(f32[3,64,16,128]{3,2,1,0:T(8,128)S(1)} %get-tuple-element.7, f32[1,64,16,128]{3,2,1,0:T(8,128)} %fusion.113, f32[1,64,16,128]{3,2,1,0:T(8,128)} %fusion.115, f32[1,64,16,128]{3,2,1,0:T(8,128)} %fusion.117, f32[3,66,18,130]{3,2,1,0:T(8,128)S(1)} %select_maximum_fusion, ...), kind=kLoop, calls=%fused_computation.254 | loop fusion | flops 24379392 | bytes 46858248 | tf_op jit(solution)/shard_map/add | solution.py:127
  (158 shorter events, 156.0 us)
Async XLA Ops:
  1.5 31.4 %collective-permute-start.4 = (f32[3,64,1,128]{3,1,2,0:T(8,128)S(1)}, f32[3,64,1,128]{3,1,2,0:T(8,128)S(1)}, u32[]{:S(2)}, u32[]{:S(2)}) collective-permute-start(f32[3,64,1,128]{3,1,2,0:T(8,128)S(1)} %bitcast.95), channel_id=1, source_target_pairs={{0,16},{16,32},{32,48},{48,64},{64,80},{80,96},{96,112},{1,17},{17... | collective-permute-start | bytes 294920 | tf_op jit(solution)/shard_map/ppermute | solution.py:24
  4.7 28.2 %collective-permute-start.5 = (f32[3,64,1,128]{3,1,2,0:T(8,128)S(1)}, f32[3,64,1,128]{3,1,2,0:T(8,128)S(1)}, u32[]{:S(2)}, u32[]{:S(2)}) collective-permute-start(f32[3,64,1,128]{3,1,2,0:T(8,128)S(1)} %bitcast.94), channel_id=1, source_target_pairs={{16,0},{32,16},{48,32},{64,48},{80,64},{96,80},{112,96},{17,1},{33... | collective-permute-start | bytes 294920 | tf_op jit(solution)/shard_map/ppermute | solution.py:26
  15.9 18.9 %all-to-all-start = ((s32[128,24,1]{1,2,0:T(1,128)}), s32[128,24,1]{1,2,0:T(1,128)S(1)}, u32[]{:S(2)}, u32[]{:S(2)}) async-start(s32[128,24,1]{1,2,0:T(1,128)} %bitcast.3), calls=%async_computation | async-start | bytes 131072 | tf_op jit(solution)/shard_map/all_to_all | solution.py:102
  34.7 51.8 %all-to-all-start.1 = ((f32[128,24,128]{2,1,0:T(8,128)}), f32[128,24,128]{2,1,0:T(8,128)S(1)}, u32[]{:S(2)}, u32[]{:S(2)}) async-start(f32[128,24,128]{2,1,0:T(8,128)} %bitcast.4), calls=%async_computation.1 | async-start | bytes 3145728 | tf_op jit(solution)/shard_map/all_to_all | solution.py:101
  52.2 14.3 %collective-permute-start.6 = (f32[3,64,18,1]{1,2,3,0:T(8,128)S(1)}, f32[3,64,18,1]{1,2,3,0:T(8,128)}, u32[]{:S(2)}, u32[]{:S(2)}) collective-permute-start(f32[3,64,18,1]{1,2,3,0:T(8,128)S(1)} %copy.90), channel_id=1, source_target_pairs={{0,1},{1,2},{2,3},{3,4},{4,5},{5,6},{6,7},{7,8},{8,9},{9,10},{10,1... | collective-permute-start | bytes 41480 | tf_op jit(solution)/shard_map/ppermute | solution.py:24
  60.7 9.2 %collective-permute-start.7 = (f32[3,64,18,1]{1,2,3,0:T(8,128)}, f32[3,64,18,1]{1,2,3,0:T(8,128)}, u32[]{:S(2)}, u32[]{:S(2)}) collective-permute-start(f32[3,64,18,1]{1,2,3,0:T(8,128)} %copy.91), channel_id=1, source_target_pairs={{1,0},{2,1},{3,2},{4,3},{5,4},{6,5},{7,6},{8,7},{9,8},{10,9},{11,1... | collective-permute-start | bytes 41480 | tf_op jit(solution)/shard_map/ppermute | solution.py:26
  108.5 10.3 %collective-permute-start = (f32[64,1,128]{2,1,0:T(1,128)S(1)}, f32[64,1,128]{2,1,0:T(1,128)S(1)}, u32[]{:S(2)}, u32[]{:S(2)}) collective-permute-start(f32[64,1,128]{2,1,0:T(1,128)S(1)} %get-tuple-element.54), channel_id=1, source_target_pairs={{0,16},{16,32},{32,48},{48,64},{64,80},{80,96},{96,112},{1,17},{17... | collective-permute-start | bytes 98312 | tf_op jit(solution)/shard_map/ppermute | solution.py:24
  110.8 8.1 %collective-permute-start.1 = (f32[64,1,128]{2,1,0:T(1,128)S(1)}, f32[64,1,128]{2,1,0:T(1,128)S(1)}, u32[]{:S(2)}, u32[]{:S(2)}) collective-permute-start(f32[64,1,128]{2,1,0:T(1,128)S(1)} %get-tuple-element.55), channel_id=1, source_target_pairs={{16,0},{32,16},{48,32},{64,48},{80,64},{96,80},{112,96},{17,1},{33... | collective-permute-start | bytes 98312 | tf_op jit(solution)/shard_map/ppermute | solution.py:26
  119.5 17.1 %collective-permute-start.2 = (f32[64,18,1]{0,2,1:T(1,128)S(1)}, f32[64,18,1]{0,2,1:T(1,128)S(1)}, u32[]{:S(2)}, u32[]{:S(2)}) collective-permute-start(f32[64,18,1]{0,2,1:T(1,128)S(1)} %copy.80), channel_id=1, source_target_pairs={{0,1},{1,2},{2,3},{3,4},{4,5},{5,6},{6,7},{7,8},{8,9},{9,10},{10,1... | collective-permute-start | bytes 13832 | tf_op jit(solution)/shard_map/ppermute | solution.py:24
  128.2 8.8 %collective-permute-start.3 = (f32[64,18,1]{0,2,1:T(1,128)S(1)}, f32[64,18,1]{0,2,1:T(1,128)S(1)}, u32[]{:S(2)}, u32[]{:S(2)}) collective-permute-start(f32[64,18,1]{0,2,1:T(1,128)S(1)} %copy.81), channel_id=1, source_target_pairs={{1,0},{2,1},{3,2},{4,3},{5,4},{6,5},{7,6},{8,7},{9,8},{10,9},{11,1... | collective-permute-start | bytes 13832 | tf_op jit(solution)/shard_map/ppermute | solution.py:26
  141.6 71.1 %copy-start.13 = (f32[1,64,16,128]{3,2,1,0:T(8,128)}, f32[1,64,16,128]{3,2,1,0:T(8,128)S(1)}, u32[]{:S(2)}) copy-start(f32[1,64,16,128]{3,2,1,0:T(8,128)S(1)} %get-tuple-element.51) | copy-start | bytes 1572868
  141.6 71.0 %copy-start.15 = (f32[1,64,16,128]{3,2,1,0:T(8,128)}, f32[1,64,16,128]{3,2,1,0:T(8,128)S(1)}, u32[]{:S(2)}) copy-start(f32[1,64,16,128]{3,2,1,0:T(8,128)S(1)} %get-tuple-element.52) | copy-start | bytes 1572868
  154.7 6.1 %collective-permute-start.8 = (f32[3,64,1,128]{3,1,2,0:T(8,128)S(1)}, f32[3,64,1,128]{3,1,2,0:T(8,128)S(1)}, u32[]{:S(2)}, u32[]{:S(2)}) collective-permute-start(f32[3,64,1,128]{3,1,2,0:T(8,128)S(1)} %bitcast.99), channel_id=1, source_target_pairs={{0,16},{16,32},{32,48},{48,64},{64,80},{80,96},{96,112},{1,17},{17... | collective-permute-start | bytes 294920 | tf_op jit(solution)/shard_map/ppermute | solution.py:24
  158.9 7.5 %collective-permute-start.9 = (f32[3,64,1,128]{3,1,2,0:T(8,128)S(1)}, f32[3,64,1,128]{3,1,2,0:T(8,128)S(1)}, u32[]{:S(2)}, u32[]{:S(2)}) collective-permute-start(f32[3,64,1,128]{3,1,2,0:T(8,128)S(1)} %bitcast.96), channel_id=1, source_target_pairs={{16,0},{32,16},{48,32},{64,48},{80,64},{96,80},{112,96},{17,1},{33... | collective-permute-start | bytes 294920 | tf_op jit(solution)/shard_map/ppermute | solution.py:26
  172.1 15.4 %collective-permute-start.10 = (f32[3,64,18,1]{1,2,3,0:T(8,128)S(1)}, f32[3,64,18,1]{1,2,3,0:T(8,128)S(1)}, u32[]{:S(2)}, u32[]{:S(2)}) collective-permute-start(f32[3,64,18,1]{1,2,3,0:T(8,128)S(1)} %copy.102), channel_id=1, source_target_pairs={{0,1},{1,2},{2,3},{3,4},{4,5},{5,6},{6,7},{7,8},{8,9},{9,10},{10,1... | collective-permute-start | bytes 41480 | tf_op jit(solution)/shard_map/ppermute | solution.py:24
  183.8 8.9 %collective-permute-start.11 = (f32[3,64,18,1]{1,2,3,0:T(8,128)S(1)}, f32[3,64,18,1]{1,2,3,0:T(8,128)S(1)}, u32[]{:S(2)}, u32[]{:S(2)}) collective-permute-start(f32[3,64,18,1]{1,2,3,0:T(8,128)S(1)} %copy.103), channel_id=1, source_target_pairs={{1,0},{2,1},{3,2},{4,3},{5,4},{6,5},{7,6},{8,7},{9,8},{10,9},{11,1... | collective-permute-start | bytes 41480 | tf_op jit(solution)/shard_map/ppermute | solution.py:26
  226.6 5.8 %collective-permute-start.12 = (f32[3,64,1,128]{3,1,2,0:T(8,128)S(1)}, f32[3,64,1,128]{3,1,2,0:T(8,128)S(1)}, u32[]{:S(2)}, u32[]{:S(2)}) collective-permute-start(f32[3,64,1,128]{3,1,2,0:T(8,128)S(1)} %bitcast.100), channel_id=1, source_target_pairs={{0,16},{16,32},{32,48},{48,64},{64,80},{80,96},{96,112},{1,17},{17... | collective-permute-start | bytes 294920 | tf_op jit(solution)/shard_map/ppermute | solution.py:24
  228.5 7.5 %collective-permute-start.13 = (f32[3,64,1,128]{3,1,2,0:T(8,128)S(1)}, f32[3,64,1,128]{3,1,2,0:T(8,128)S(1)}, u32[]{:S(2)}, u32[]{:S(2)}) collective-permute-start(f32[3,64,1,128]{3,1,2,0:T(8,128)S(1)} %bitcast.97), channel_id=1, source_target_pairs={{16,0},{32,16},{48,32},{64,48},{80,64},{96,80},{112,96},{17,1},{33... | collective-permute-start | bytes 294920 | tf_op jit(solution)/shard_map/ppermute | solution.py:26
  242.4 8.1 %collective-permute-start.14 = (f32[3,64,18,1]{1,2,3,0:T(8,128)S(1)}, f32[3,64,18,1]{1,2,3,0:T(8,128)S(1)}, u32[]{:S(2)}, u32[]{:S(2)}) collective-permute-start(f32[3,64,18,1]{1,2,3,0:T(8,128)S(1)} %copy.114), channel_id=1, source_target_pairs={{0,1},{1,2},{2,3},{3,4},{4,5},{5,6},{6,7},{7,8},{8,9},{9,10},{10,1... | collective-permute-start | bytes 41480 | tf_op jit(solution)/shard_map/ppermute | solution.py:24
  248.5 8.9 %collective-permute-start.15 = (f32[3,64,18,1]{1,2,3,0:T(8,128)S(1)}, f32[3,64,18,1]{1,2,3,0:T(8,128)S(1)}, u32[]{:S(2)}, u32[]{:S(2)}) collective-permute-start(f32[3,64,18,1]{1,2,3,0:T(8,128)S(1)} %copy.115), channel_id=1, source_target_pairs={{1,0},{2,1},{3,2},{4,3},{5,4},{6,5},{7,6},{8,7},{9,8},{10,9},{11,1... | collective-permute-start | bytes 41480 | tf_op jit(solution)/shard_map/ppermute | solution.py:26
  290.0 5.5 %collective-permute-start.16 = (f32[3,64,1,128]{3,1,2,0:T(8,128)S(1)}, f32[3,64,1,128]{3,1,2,0:T(8,128)S(1)}, u32[]{:S(2)}, u32[]{:S(2)}) collective-permute-start(f32[3,64,1,128]{3,1,2,0:T(8,128)S(1)} %bitcast.101), channel_id=1, source_target_pairs={{0,16},{16,32},{32,48},{48,64},{64,80},{80,96},{96,112},{1,17},{17... | collective-permute-start | bytes 294920 | tf_op jit(solution)/shard_map/ppermute | solution.py:24
  291.9 7.5 %collective-permute-start.17 = (f32[3,64,1,128]{3,1,2,0:T(8,128)S(1)}, f32[3,64,1,128]{3,1,2,0:T(8,128)S(1)}, u32[]{:S(2)}, u32[]{:S(2)}) collective-permute-start(f32[3,64,1,128]{3,1,2,0:T(8,128)S(1)} %bitcast.98), channel_id=1, source_target_pairs={{16,0},{32,16},{48,32},{64,48},{80,64},{96,80},{112,96},{17,1},{33... | collective-permute-start | bytes 294920 | tf_op jit(solution)/shard_map/ppermute | solution.py:26
  305.1 8.2 %collective-permute-start.18 = (f32[3,64,18,1]{1,2,3,0:T(8,128)S(1)}, f32[3,64,18,1]{1,2,3,0:T(8,128)S(1)}, u32[]{:S(2)}, u32[]{:S(2)}) collective-permute-start(f32[3,64,18,1]{1,2,3,0:T(8,128)S(1)} %copy.126), channel_id=1, source_target_pairs={{0,1},{1,2},{2,3},{3,4},{4,5},{5,6},{6,7},{7,8},{8,9},{9,10},{10,1... | collective-permute-start | bytes 41480 | tf_op jit(solution)/shard_map/ppermute | solution.py:24
  311.2 8.9 %collective-permute-start.19 = (f32[3,64,18,1]{1,2,3,0:T(8,128)S(1)}, f32[3,64,18,1]{1,2,3,0:T(8,128)S(1)}, u32[]{:S(2)}, u32[]{:S(2)}) collective-permute-start(f32[3,64,18,1]{1,2,3,0:T(8,128)S(1)} %copy.127), channel_id=1, source_target_pairs={{1,0},{2,1},{3,2},{4,3},{5,4},{6,5},{7,6},{8,7},{9,8},{10,9},{11,1... | collective-permute-start | bytes 41480 | tf_op jit(solution)/shard_map/ppermute | solution.py:26
  (26 other events, 165.7 us)
where the time goes:
time: 359 us; the launch traced here: 352 us
  other arithmetic  159 us (44%)
  starting transfers between devices  91.4 us (25%)
  local copies, waits for them, and re-layouts  72 us (20%)
  waiting for transfers between devices  26.1 us (7%)
  between operations  3.81 us (1%)
    add x4, other arithmetic, local(): field = field + step_field  49.9 us
    concatenate x14, other arithmetic, with_halo(): jnp.concatenate([lax.ppermute(tail, axis, [(i, (i + 1) % count) for i in...  49.3 us
    ppermute x10, starting transfers between devices, with_halo(): lax.ppermute(tail, axis, [(i, (i + 1) % count) for i in range(ends)])  45.7 us
    add x12, other arithmetic, operate(): summed = summed + 0.25 * (plus_plus - plus_minus - minus_plus + minus_minus)  34.2 us
    ppermute x10, waiting for transfers between devices, with_halo(): lax.ppermute(head, axis, [((i + 1) % count, i) for i in range(ends)])  26.1 us
    ppermute x10, starting transfers between devices, with_halo(): lax.ppermute(head, axis, [((i + 1) % count, i) for i in range(ends)])  24.9 us
    slice x10, local copies, waits for them, and re-layouts, with_halo(): head = lax.slice_in_dim(cells, 0, width, axis=dim)  22.4 us
    scatter-add x1, other arithmetic, local(): jax.ops.segment_sum(got_rows, got_ids, num_segments=elements + 1)  17.4 us
  transfers between devices with their start and end apart: 22, of which 7 were waited for; matrix products, arithmetic and copies ran while one was open for 21% of the time, Pallas kernels for 0%

commit v1 on v0

--- a/solution.py
+++ b/solution.py
@@ -1,6 +1,10 @@
+import functools
+
 import jax
 import jax.numpy as jnp
 from jax import lax
+from jax.experimental import pallas as pl
+from jax.experimental.pallas import tpu as pltpu
 from jax.sharding import PartitionSpec as P
 
 SWEEPS = 4
@@ -81,28 +85,208 @@
     ratio_next = 1.0 / (2.0 * sigma - ratio_now)
     return (ratio_next * ratio_now * step_prev + 2.0 * ratio_next / delta * scaled, ratio_next)
 
+MESH = pl.DeviceIdType.MESH
+
+
+def halves(values):
+    high = values.astype(jnp.bfloat16)
+    low = (values - high.astype(jnp.float32)).astype(jnp.bfloat16)
+    return high, low
+
+
+def onehot(matches):
+    return jnp.where(matches, 1.0, 0.0).astype(jnp.bfloat16)
+
+
+def exchange_kernel(
+    nx, ny, owner_ref, element_ref, rows_ref, out_ref,
+    split_ref, place_ref, send_rows, send_ids, got_rows, got_ids, total,
+    ids_send_sem, ids_recv_sem, rows_send_sem, rows_recv_sem,
+):
+    tiles = nx * ny
+    count = rows_ref.shape[0]
+    length = rows_ref.shape[1]
+    elements = out_ref.shape[0]
+    group = ny * CAP
+    gx = lax.axis_index("gx")
+    gy = lax.axis_index("gy")
+
+    def there(step):
+        return lax.rem(gx + step // ny, nx), lax.rem(gy + lax.rem(step, ny), ny)
+
+    barrier = pltpu.get_barrier_semaphore()
+
+    def greet(step, carry):
+        pl.semaphore_signal(barrier, inc=1, device_id=there(step), device_id_type=MESH)
+        return carry
+
+    lax.fori_loop(1, tiles, greet, 0)
+
+    owner = owner_ref[...]
+    element = element_ref[...] + 1
+    tile_of = lax.broadcasted_iota(jnp.int32, (tiles, count), 0)
+    member = jnp.where(tile_of == owner, 1.0, 0.0)
+    member16 = member.astype(jnp.bfloat16)
+    block = 256
+    earlier = onehot(
+        lax.broadcasted_iota(jnp.int32, (block, block), 0) < lax.broadcasted_iota(jnp.int32, (block, block), 1)
+    )
+    carry = jnp.zeros((tiles, 1), jnp.float32)
+    slots = []
+    for first in range(0, count, block):
+        part = member[:, first : first + block]
+        before = jnp.dot(member16[:, first : first + block], earlier, preferred_element_type=jnp.float32) + carry
+        slots.append(jnp.sum(before * part, axis=0, keepdims=True))
+        carry = carry + jnp.sum(part, axis=1, keepdims=True)
+    slot = jnp.concatenate(slots, axis=1).astype(jnp.int32)
+    place_ref[...] = owner * CAP + slot
+
+    weighed = jnp.concatenate(
+        [
+            (member * (element // 32).astype(jnp.float32)).astype(jnp.bfloat16),
+            (member * lax.rem(element, 32).astype(jnp.float32)).astype(jnp.bfloat16),
+        ],
+        axis=0,
+    )
+    slot_of = onehot(lax.broadcasted_iota(jnp.int32, (length, count), 0) == slot)
+    both = lax.dot_general(weighed, slot_of, (((1,), (1,)), ((), ())), preferred_element_type=jnp.float32)
+    send_ids[...] = (32.0 * both[:tiles] + both[tiles:]).reshape(tiles, 1, length)
+
+    high, low = halves(rows_ref[...])
+    split_ref[:, :length] = high
+    split_ref[:, length:] = low
+
+    pl.semaphore_wait(barrier, tiles - 1)
+
+    def number(device):
+        return device[0] * ny + device[1]
+
+    def send_id(step, carry):
+        to = there(step)
+        pltpu.make_async_remote_copy(
+            src_ref=send_ids.at[number(to)],
+            dst_ref=got_ids.at[step],
+            send_sem=ids_send_sem,
+            recv_sem=ids_recv_sem,
+            device_id=to,
+            device_id_type=MESH,
+        ).start()
+        return carry
+
+    lax.fori_loop(1, tiles, send_id, 0)
+    got_ids[0] = send_ids[number((gx, gy))]
+
+    def pack(turn, carry):
+        tile_x = lax.rem(gx + turn, nx)
+        base = tile_x * group
+        wanted = base + lax.broadcasted_iota(jnp.int32, (group, count), 0)
+        pick = onehot(wanted == place_ref[...])
+        picked = jnp.dot(pick, split_ref[...], preferred_element_type=jnp.float32)
+        packed = (picked[:, :length] + picked[:, length:]).reshape(ny, CAP, length)
+        send_rows[pl.ds(tile_x * ny, ny)] = packed
+
+        def send(turn_y, carry):
+            tile_y = lax.rem(gy + turn_y, ny)
+            pltpu.make_async_remote_copy(
+                src_ref=send_rows.at[tile_x * ny + tile_y],
+                dst_ref=got_rows.at[turn * ny + turn_y],
+                send_sem=rows_send_sem,
+                recv_sem=rows_recv_sem.at[turn],
+                device_id=(tile_x, tile_y),
+                device_id_type=MESH,
+            ).start()
+            return carry
+
+        @pl.when(turn == 0)
+        def _():
+            lax.fori_loop(1, ny, send, 0)
+
+        @pl.when(turn > 0)
+        def _():
+            lax.fori_loop(0, ny, send, 0)
+
+        return carry
+
+    lax.fori_loop(0, nx, pack, 0)
+    got_rows[0] = send_rows[number((gx, gy))]
+
+    rest = pl.ds(1, tiles - 1)
+    pltpu.make_async_copy(got_ids.at[rest], got_ids.at[rest], ids_recv_sem).wait()
+
+    spread = onehot(
+        lax.broadcasted_iota(jnp.int32, (length, group), 0)
+        == lax.rem(lax.broadcasted_iota(jnp.int32, (length, group), 1), CAP)
+    )
+    own_lane = lax.broadcasted_iota(jnp.int32, (ny, group), 0) == lax.broadcasted_iota(jnp.int32, (ny, group), 1) // CAP
+    total[...] = jnp.zeros_like(total)
+
+    def collect(turn, carry):
+        @pl.when(turn == 0)
+        def _():
+            part = got_rows.at[pl.ds(1, ny - 1)]
+            pltpu.make_async_copy(part, part, rows_recv_sem.at[0]).wait()
+
+        @pl.when(turn > 0)
+        def _():
+            part = got_rows.at[pl.ds(turn * ny, ny)]
+            pltpu.make_async_copy(part, part, rows_recv_sem.at[turn]).wait()
+
+        ids = got_ids[pl.ds(turn * ny, ny)].reshape(ny, length)
+        ids_high = jnp.floor(ids * (1.0 / 32.0))
+        ids_low = ids - 32.0 * ids_high
+        wide = 32.0 * jnp.dot(ids_high.astype(jnp.bfloat16), spread, preferred_element_type=jnp.float32) + jnp.dot(
+            ids_low.astype(jnp.bfloat16), spread, preferred_element_type=jnp.float32
+        )
+        flat = jnp.sum(jnp.where(own_lane, wide, 0.0), axis=0, keepdims=True).astype(jnp.int32) - 1
+        place = onehot(lax.broadcasted_iota(jnp.int32, (elements, group), 0) == flat)
+        high, low = halves(got_rows[pl.ds(turn * ny, ny)].reshape(group, length))
+        total[...] += jnp.dot(place, jnp.concatenate([high, low], axis=1), preferred_element_type=jnp.float32)
+        return carry
+
+    lax.fori_loop(0, nx, collect, 0)
+    out_ref[...] = total[:, :length] + total[:, length:]
+
+    pltpu.make_async_copy(send_ids.at[rest], send_ids.at[rest], ids_send_sem).wait()
+    pltpu.make_async_copy(send_rows.at[rest], send_rows.at[rest], rows_send_sem).wait()
+
+
+def exchange(owner, element, rows, elements):
+    nx, ny = lax.axis_size("gx"), lax.axis_size("gy")
+    tiles = nx * ny
+    count, length = rows.shape
+    return pl.pallas_call(
+        functools.partial(exchange_kernel, nx, ny),
+        out_shape=jax.ShapeDtypeStruct((elements, length), jnp.float32),
+        in_specs=[pl.BlockSpec(memory_space=pltpu.VMEM)] * 3,
+        out_specs=pl.BlockSpec(memory_space=pltpu.VMEM),
+        scratch_shapes=[
+            pltpu.VMEM((count, 2 * length), jnp.bfloat16),
+            pltpu.VMEM((1, count), jnp.int32),
+            pltpu.VMEM((tiles, CAP, length), jnp.float32),
+            pltpu.VMEM((tiles, 1, length), jnp.float32),
+            pltpu.VMEM((tiles, CAP, length), jnp.float32),
+            pltpu.VMEM((tiles, 1, length), jnp.float32),
+            pltpu.VMEM((elements, 2 * length), jnp.float32),
+            pltpu.SemaphoreType.DMA,
+            pltpu.SemaphoreType.DMA,
+            pltpu.SemaphoreType.DMA,
+            pltpu.SemaphoreType.DMA((nx,)),
+        ],
+        compiler_params=pltpu.CompilerParams(
+            collective_id=0, has_side_effects=True, vmem_limit_bytes=40 * 1024 * 1024
+        ),
+        name="exchange",
+    )(owner, element, rows)
+
 
 def local(thermal_rows, row_owner, row_element, modulus, birth, start_disp, bounds):
-    tiles_x = lax.axis_size("gx")
-    tiles_y = lax.axis_size("gy")
-    tiles = tiles_x * tiles_y
     depth = modulus.shape[0]
     breadth = modulus.shape[1]
     length = modulus.shape[2]
     elements = depth * breadth
-    owner = row_owner[:, 0]
-    onehot = (owner[:, None] == jnp.arange(tiles, dtype=jnp.int32)[None, :]).astype(jnp.int32)
-    before = jnp.cumsum(onehot, axis=0) - onehot
-    slot = jnp.sum(before * onehot, axis=1)
-    position = owner * CAP + slot
-    send_rows = jnp.zeros((tiles * CAP, length), jnp.float32).at[position].set(thermal_rows)
-    send_ids = jnp.full((tiles * CAP,), elements, jnp.int32).at[position].set(row_element[:, 0])
-    got_rows, got_ids = (
-        lax.all_to_all(send_rows, ("gx", "gy"), split_axis=0, concat_axis=0, tiled=True),
-        lax.all_to_all(send_ids, ("gx", "gy"), split_axis=0, concat_axis=0, tiled=True),
-    )
-    summed_rows = jax.ops.segment_sum(got_rows, got_ids, num_segments=elements + 1)
-    increment = summed_rows[:elements].reshape(depth, breadth, length)
+    count = thermal_rows.shape[0]
+    summed_rows = exchange(row_owner.reshape(1, count), row_element.reshape(1, count), thermal_rows, elements)
+    increment = summed_rows.reshape(depth, breadth, length)
     stress = modulus * increment
     lower = bounds[0]
     upper = bounds[1]

time: 359 us -> 385 us (1.072)
  other arithmetic: 159 us -> 197 us
  Pallas kernels: 0 us -> 35.6 us
  local copies, waits for them, and re-layouts: 72 us -> 48.4 us
  starting transfers between devices: 91.4 us -> 71.9 us
  waiting for transfers between devices: 26.1 us -> 21.4 us
    add x4, other arithmetic: 49.9 us -> 149 us  [local(): field = field + step_field]
    pallas_call x0 -> x1, Pallas kernels: none -> 35.6 us  [exchange(): pl.pallas_call(functools.partial(exchange_kernel, nx, ny), out_shape=jax....]
    concatenate x14, other arithmetic: 49.3 us -> 23 us  [with_halo(): jnp.concatenate([lax.ppermute(tail, axis, [(i, (i + 1) % count) for i in...]
    all_to_all x2 -> x0, starting transfers between devices: 20.9 us -> none  [the longest x1 11.1 us: local(): lax.all_to_all(send_ids, ('gx', 'gy'), split_axis=0, concat_axis=0, tiled...]
    slice x10 -> x7, local copies, waits for them, and re-layouts: 22.4 us -> 2.19 us  [with_halo(): head = lax.slice_in_dim(cells, 0, width, axis=dim)]
    scatter-add x1 -> x0, other arithmetic: 17.4 us -> none  [local(): jax.ops.segment_sum(got_rows, got_ids, num_segments=elements + 1)]
    mul x0 -> x7, local copies, waits for them, and re-layouts: none -> 17 us  [the longest x4 9.95 us: local(): modulus * jnp.where(birth <= sweep, 1.0, SOFTENED).astype(jnp.float32)]
    add x12 -> x8, other arithmetic: 34.2 us -> 20.7 us  [operate(): summed = summed + 0.25 * (plus_plus - plus_minus - minus_plus + minus_minus)]
  transfers between devices with their start and end apart: 22 -> 20, of which waited for: 7 -> 9; matrix products, arithmetic and copies ran while one was open for 21% -> 10% of each run, Pallas kernels for 0% -> 9%
where the time goes in v1:
time: 385 us; the launch traced here: 379 us
  other arithmetic  197 us (51%)
  starting transfers between devices  71.9 us (19%)
  local copies, waits for them, and re-layouts  48.4 us (13%)
  Pallas kernels  35.6 us (9%)
  waiting for transfers between devices  21.4 us (6%)
  between operations  3.9 us (1%)
    add x4, other arithmetic, local(): field = field + step_field  149 us
    ppermute x10, starting transfers between devices, with_halo(): lax.ppermute(tail, axis, [(i, (i + 1) % count) for i in range(ends)])  45.8 us
    pallas_call x1, Pallas kernels, exchange(): pl.pallas_call(functools.partial(exchange_kernel, nx, ny), out_shape=jax....  35.6 us
    ppermute x10, starting transfers between devices, with_halo(): lax.ppermute(head, axis, [((i + 1) % count, i) for i in range(ends)])  26 us
    concatenate x14, other arithmetic, with_halo(): jnp.concatenate([lax.ppermute(tail, axis, [(i, (i + 1) % count) for i in...  23 us
    ppermute x10, waiting for transfers between devices, with_halo(): lax.ppermute(head, axis, [((i + 1) % count, i) for i in range(ends)])  21.1 us
    add x8, other arithmetic, operate(): summed = summed + 0.25 * (plus_plus - plus_minus - minus_plus + minus_minus)  20.7 us
    mul x4, local copies, waits for them, and re-layouts, local(): modulus * jnp.where(birth <= sweep, 1.0, SOFTENED).astype(jnp.float32)  9.95 us
  transfers between devices with their start and end apart: 20, of which 9 were waited for; matrix products, arithmetic and copies ran while one was open for 10% of the time, Pallas kernels for 9%

profile of v1, /device:TPU:31, one launch (start us, length us, event | category | flops | bytes accessed | tf_op | source)
XLA Modules:
  0.0 378.5 jit_solution(17196095318233173023)
XLA Ops:
  1.5 3.2 collective-permute-start.4
  9.3 35.6 %exchange.1 = f32[1024,128]{1,0:T(8,128)S(1)} custom-call(s32[1,1536]{1,0:T(1,128)S(1)} %bitcast.15, s32[1,1536]{1,0:T(1,128)S(1)} %bitcast.16, f32[1536,128]{1,0:T(8,128)S(1)} %copy-done), custom_call_target="tpu_custom_call" | custom-call | tf_op jit(solution)/shard_map/exchange/pallas_call | solution.py:257
  48.1 3.1 collective-permute-start.1
  55.2 7.9 %collective-permute-start.2 = (f32[64,18,1]{0,2,1:T(1,128)S(1)}, f32[64,18,1]{0,2,1:T(1,128)S(1)}, u32[]{:S(2)}, u32[]{:S(2)}) collective-permute-start(f32[64,18,1]{0,2,1:T(1,128)S(1)} %get-tuple-element.54), channel_id=1, source_target_pairs={{0,1},{1,2},{2,3},{3,4},{4,5},{5,6},{6,7},{7,8},{8,9},{9,10},{10,1... | collective-permute-start | bytes 13832 | tf_op jit(solution)/shard_map/ppermute | solution.py:28
  79.3 7.4 %collective-permute-start.6 = (f32[3,64,18,1]{1,2,3,0:T(8,128)S(1)}, f32[3,64,18,1]{1,2,3,0:T(8,128)S(1)}, u32[]{:S(2)}, u32[]{:S(2)}) collective-permute-start(f32[3,64,18,1]{1,2,3,0:T(8,128)S(1)} %copy.17), channel_id=1, source_target_pairs={{0,1},{1,2},{2,3},{3,4},{4,5},{5,6},{6,7},{7,8},{8,9},{9,10},{10,1... | collective-permute-start | bytes 41480 | tf_op jit(solution)/shard_map/ppermute | solution.py:28
  91.2 4.3 %collective-permute-done.7 = f32[3,64,18,1]{1,2,3,0:T(8,128)S(1)} collective-permute-done((f32[3,64,18,1]{1,2,3,0:T(8,128)S(1)}, f32[3,64,18,1]{1,2,3,0:T(8,128)S(1)}, u32[]{:S(2)}, u32[]{:S(2)}) %collective-permute-start.7) | collective-permute-done | bytes 13856 | tf_op jit(solution)/shard_map/ppermute | solution.py:30
  97.6 2.8 select_maximum_fusion.12
  105.3 37.7 %fusion.140 = (f32[3,64,16,128]{1,3,2,0:T(8,128)S(1)}, f32[3,64,16,128]{1,3,2,0:T(8,128)}) fusion(f32[3,64,16,128]{1,3,2,0:T(8,128)} %copy-done.16, f32[64,16,128]{0,2,1:T(8,128)} %copy.27, f32[1,64,16,128]{1,3,2,0:T(8,128)} %get-tuple-element.26, f32[1,64,16,128]{1,3,2,0:T(8,128)} %get-tuple-element.25, f32[1,64,16,128]{1,3,2,0:T(8,128)} %fusion.129, ...), kind=kLoop, calls=%fused_computation.388 | loop fusion | flops 23199744 | bytes 46858240 | tf_op jit(solution)/shard_map/add | solution.py:311
  145.8 3.4 collective-permute-start.9
  149.4 3.9 %collective-permute-done.9 = f32[3,64,1,128]{3,1,2,0:T(8,128)} collective-permute-done((f32[3,64,1,128]{3,1,2,0:T(8,128)S(1)}, f32[3,64,1,128]{3,1,2,0:T(8,128)}, u32[]{:S(2)}, u32[]{:S(2)}) %collective-permute-start.9) | collective-permute-done | bytes 98336 | tf_op jit(solution)/shard_map/ppermute | solution.py:30
  155.0 4.1 %collective-permute-start.10 = (f32[3,64,18,1]{1,2,3,0:T(8,128)}, f32[3,64,18,1]{1,2,3,0:T(8,128)}, u32[]{:S(2)}, u32[]{:S(2)}) collective-permute-start(f32[3,64,18,1]{1,2,3,0:T(8,128)} %copy.34), channel_id=1, source_target_pairs={{0,1},{1,2},{2,3},{3,4},{4,5},{5,6},{6,7},{7,8},{8,9},{9,10},{10,1... | collective-permute-start | bytes 41480 | tf_op jit(solution)/shard_map/ppermute | solution.py:28
  170.0 2.8 select_maximum_fusion.8
  180.7 36.2 %fusion.139 = (f32[3,64,16,128]{1,3,2,0:T(8,128)}, f32[3,64,16,128]{1,3,2,0:T(8,128)}) fusion(f32[3,64,16,128]{1,3,2,0:T(8,128)S(1)} %get-tuple-element.15, f32[64,16,128]{0,2,1:T(8,128)} %copy.42, f32[1,64,16,128]{1,3,2,0:T(8,128)} %get-tuple-element.24, f32[1,64,16,128]{1,3,2,0:T(8,128)} %get-tuple-element.23, f32[1,64,16,128]{1,3,2,0:T(8,128)} %fusion.123, ...), kind=kLoop, calls=%fused_computation.387 | loop fusion | flops 24379392 | bytes 48431112 | tf_op jit(solution)/shard_map/add | solution.py:311
  220.1 3.4 collective-permute-start.13
  223.6 4.0 %collective-permute-done.13 = f32[3,64,1,128]{3,1,2,0:T(8,128)S(1)} collective-permute-done((f32[3,64,1,128]{3,1,2,0:T(8,128)S(1)}, f32[3,64,1,128]{3,1,2,0:T(8,128)S(1)}, u32[]{:S(2)}, u32[]{:S(2)}) %collective-permute-start.13) | collective-permute-done | bytes 98336 | tf_op jit(solution)/shard_map/ppermute | solution.py:30
  229.6 8.4 %collective-permute-start.14 = (f32[3,64,18,1]{1,2,3,0:T(8,128)}, f32[3,64,18,1]{1,2,3,0:T(8,128)}, u32[]{:S(2)}, u32[]{:S(2)}) collective-permute-start(f32[3,64,18,1]{1,2,3,0:T(8,128)} %copy.48), channel_id=1, source_target_pairs={{0,1},{1,2},{2,3},{3,4},{4,5},{5,6},{6,7},{7,8},{8,9},{9,10},{10,1... | collective-permute-start | bytes 41480 | tf_op jit(solution)/shard_map/ppermute | solution.py:28
  248.6 2.8 select_maximum_fusion.4
  259.3 39.0 %fusion.138 = (f32[3,64,16,128]{1,3,2,0:T(8,128)S(1)}, f32[3,64,16,128]{1,3,2,0:T(8,128)}) fusion(f32[3,64,16,128]{1,3,2,0:T(8,128)} %get-tuple-element.11, f32[64,16,128]{0,2,1:T(8,128)} %copy.56, f32[1,64,16,128]{1,3,2,0:T(8,128)} %get-tuple-element.22, f32[1,64,16,128]{1,3,2,0:T(8,128)} %get-tuple-element.21, f32[1,64,16,128]{1,3,2,0:T(8,128)} %fusion.117, ...), kind=kLoop, calls=%fused_computation.386 | loop fusion | flops 24379392 | bytes 48431112 | tf_op jit(solution)/shard_map/add | solution.py:311
  301.2 3.4 collective-permute-start.17
  304.8 3.9 %collective-permute-done.17 = f32[3,64,1,128]{3,1,2,0:T(8,128)} collective-permute-done((f32[3,64,1,128]{3,1,2,0:T(8,128)S(1)}, f32[3,64,1,128]{3,1,2,0:T(8,128)}, u32[]{:S(2)}, u32[]{:S(2)}) %collective-permute-start.17) | collective-permute-done | bytes 98336 | tf_op jit(solution)/shard_map/ppermute | solution.py:30
  310.4 7.0 %collective-permute-start.18 = (f32[3,64,18,1]{1,2,3,0:T(8,128)}, f32[3,64,18,1]{1,2,3,0:T(8,128)}, u32[]{:S(2)}, u32[]{:S(2)}) collective-permute-start(f32[3,64,18,1]{1,2,3,0:T(8,128)} %copy.62), channel_id=1, source_target_pairs={{0,1},{1,2},{2,3},{3,4},{4,5},{5,6},{6,7},{7,8},{8,9},{9,10},{10,1... | collective-permute-start | bytes 41480 | tf_op jit(solution)/shard_map/ppermute | solution.py:28
  328.0 2.8 select_maximum_fusion
  338.8 36.3 %add_add_fusion = f32[3,64,16,128]{1,3,2,0:T(8,128)} fusion(f32[3,64,16,128]{1,3,2,0:T(8,128)S(1)} %get-tuple-element.7, f32[1,64,16,128]{1,3,2,0:T(8,128)} %get-tuple-element.20, f32[1,64,16,128]{1,3,2,0:T(8,128)} %get-tuple-element.19, f32[1,64,16,128]{1,3,2,0:T(8,128)} %fusion.111, f32[3,66,18,130]{1,3,2,0:T(8,128)} %copy-done.3, ...), kind=kLoop, calls=%fused_computation.240 | loop fusion | flops 24379392 | bytes 46858248 | tf_op jit(solution)/shard_map/add | solution.py:311
  375.1 3.2 copy.71
  (152 shorter events, 108.1 us)
Async XLA Ops:
  1.5 75.6 %collective-permute-start.4 = (f32[3,64,1,128]{3,1,2,0:T(8,128)S(1)}, f32[3,64,1,128]{3,1,2,0:T(8,128)}, u32[]{:S(2)}, u32[]{:S(2)}) collective-permute-start(f32[3,64,1,128]{3,1,2,0:T(8,128)S(1)} %bitcast.18), channel_id=1, source_target_pairs={{0,16},{16,32},{32,48},{48,64},{64,80},{80,96},{96,112},{1,17},{17... | collective-permute-start | bytes 294920 | tf_op jit(solution)/shard_map/ppermute | solution.py:28
  4.7 73.4 %collective-permute-start.5 = (f32[3,64,1,128]{3,1,2,0:T(8,128)S(1)}, f32[3,64,1,128]{3,1,2,0:T(8,128)}, u32[]{:S(2)}, u32[]{:S(2)}) collective-permute-start(f32[3,64,1,128]{3,1,2,0:T(8,128)S(1)} %bitcast.17), channel_id=1, source_target_pairs={{16,0},{32,16},{48,32},{64,48},{80,64},{96,80},{112,96},{17,1},{33... | collective-permute-start | bytes 294920 | tf_op jit(solution)/shard_map/ppermute | solution.py:30
  9.3 36.0 %copy-start.20 = (f32[64,16,128]{2,1,0:T(8,128)S(1)}, f32[64,16,128]{2,1,0:T(8,128)}, u32[]{:S(2)}) copy-start(f32[64,16,128]{2,1,0:T(8,128)} %param.10) | copy-start | bytes 1572868
  45.9 7.2 %collective-permute-start = (f32[64,1,128]{0,2,1:T(8,128)S(1)}, f32[64,1,128]{0,2,1:T(8,128)S(1)}, u32[]{:S(2)}, u32[]{:S(2)}) collective-permute-start(f32[64,1,128]{0,2,1:T(8,128)S(1)} %get-tuple-element.61), channel_id=1, source_target_pairs={{0,16},{16,32},{32,48},{48,64},{64,80},{80,96},{96,112},{1,17},{17... | collective-permute-start | bytes 98312 | tf_op jit(solution)/shard_map/ppermute | solution.py:28
  48.1 7.1 %collective-permute-start.1 = (f32[64,1,128]{0,2,1:T(8,128)S(1)}, f32[64,1,128]{0,2,1:T(8,128)S(1)}, u32[]{:S(2)}, u32[]{:S(2)}) collective-permute-start(f32[64,1,128]{0,2,1:T(8,128)S(1)} %get-tuple-element.62), channel_id=1, source_target_pairs={{16,0},{32,16},{48,32},{64,48},{80,64},{96,80},{112,96},{17,1},{33... | collective-permute-start | bytes 98312 | tf_op jit(solution)/shard_map/ppermute | solution.py:30
  53.1 21.2 %copy-start.21 = (f32[64,1,128]{0,2,1:T(8,128)}, f32[64,1,128]{0,2,1:T(8,128)S(1)}, u32[]{:S(2)}) copy-start(f32[64,1,128]{0,2,1:T(8,128)S(1)} %collective-permute-done) | copy-start | bytes 98308
  55.2 19.1 %collective-permute-start.2 = (f32[64,18,1]{0,2,1:T(1,128)S(1)}, f32[64,18,1]{0,2,1:T(1,128)S(1)}, u32[]{:S(2)}, u32[]{:S(2)}) collective-permute-start(f32[64,18,1]{0,2,1:T(1,128)S(1)} %get-tuple-element.54), channel_id=1, source_target_pairs={{0,1},{1,2},{2,3},{3,4},{4,5},{5,6},{6,7},{7,8},{8,9},{9,10},{10,1... | collective-permute-start | bytes 13832 | tf_op jit(solution)/shard_map/ppermute | solution.py:28
  63.1 11.3 %collective-permute-start.3 = (f32[64,18,1]{0,2,1:T(1,128)S(1)}, f32[64,18,1]{0,2,1:T(1,128)S(1)}, u32[]{:S(2)}, u32[]{:S(2)}) collective-permute-start(f32[64,18,1]{0,2,1:T(1,128)S(1)} %get-tuple-element.53), channel_id=1, source_target_pairs={{1,0},{2,1},{3,2},{4,3},{5,4},{6,5},{7,6},{8,7},{9,8},{10,9},{11,1... | collective-permute-start | bytes 13832 | tf_op jit(solution)/shard_map/ppermute | solution.py:30
  69.3 28.3 %copy-start.16 = (f32[3,64,16,128]{1,3,2,0:T(8,128)}, f32[3,64,16,128]{1,3,2,0:T(8,128)S(1)}, u32[]{:S(2)}) copy-start(f32[3,64,16,128]{1,3,2,0:T(8,128)S(1)} %copy.28) | copy-start | bytes 4718596
  79.3 11.9 %collective-permute-start.6 = (f32[3,64,18,1]{1,2,3,0:T(8,128)S(1)}, f32[3,64,18,1]{1,2,3,0:T(8,128)S(1)}, u32[]{:S(2)}, u32[]{:S(2)}) collective-permute-start(f32[3,64,18,1]{1,2,3,0:T(8,128)S(1)} %copy.17), channel_id=1, source_target_pairs={{0,1},{1,2},{2,3},{3,4},{4,5},{5,6},{6,7},{7,8},{8,9},{9,10},{10,1... | collective-permute-start | bytes 41480 | tf_op jit(solution)/shard_map/ppermute | solution.py:28
  86.7 8.9 %collective-permute-start.7 = (f32[3,64,18,1]{1,2,3,0:T(8,128)S(1)}, f32[3,64,18,1]{1,2,3,0:T(8,128)S(1)}, u32[]{:S(2)}, u32[]{:S(2)}) collective-permute-start(f32[3,64,18,1]{1,2,3,0:T(8,128)S(1)} %copy.18), channel_id=1, source_target_pairs={{1,0},{2,1},{3,2},{4,3},{5,4},{6,5},{7,6},{8,7},{9,8},{10,9},{11,1... | collective-permute-start | bytes 41480 | tf_op jit(solution)/shard_map/ppermute | solution.py:30
  143.7 5.6 %collective-permute-start.8 = (f32[3,64,1,128]{3,1,2,0:T(8,128)}, f32[3,64,1,128]{3,1,2,0:T(8,128)S(1)}, u32[]{:S(2)}, u32[]{:S(2)}) collective-permute-start(f32[3,64,1,128]{3,1,2,0:T(8,128)} %copy.30), channel_id=1, source_target_pairs={{0,16},{16,32},{32,48},{48,64},{64,80},{80,96},{96,112},{1,17},{17... | collective-permute-start | bytes 294920 | tf_op jit(solution)/shard_map/ppermute | solution.py:28
  145.8 7.6 %collective-permute-start.9 = (f32[3,64,1,128]{3,1,2,0:T(8,128)S(1)}, f32[3,64,1,128]{3,1,2,0:T(8,128)}, u32[]{:S(2)}, u32[]{:S(2)}) collective-permute-start(f32[3,64,1,128]{3,1,2,0:T(8,128)S(1)} %copy.31), channel_id=1, source_target_pairs={{16,0},{32,16},{48,32},{64,48},{80,64},{96,80},{112,96},{17,1},{33... | collective-permute-start | bytes 294920 | tf_op jit(solution)/shard_map/ppermute | solution.py:30
  155.0 13.4 %collective-permute-start.10 = (f32[3,64,18,1]{1,2,3,0:T(8,128)}, f32[3,64,18,1]{1,2,3,0:T(8,128)}, u32[]{:S(2)}, u32[]{:S(2)}) collective-permute-start(f32[3,64,18,1]{1,2,3,0:T(8,128)} %copy.34), channel_id=1, source_target_pairs={{0,1},{1,2},{2,3},{3,4},{4,5},{5,6},{6,7},{7,8},{8,9},{9,10},{10,1... | collective-permute-start | bytes 41480 | tf_op jit(solution)/shard_map/ppermute | solution.py:28
  159.7 9.5 %collective-permute-start.11 = (f32[3,64,18,1]{1,2,3,0:T(8,128)}, f32[3,64,18,1]{1,2,3,0:T(8,128)}, u32[]{:S(2)}, u32[]{:S(2)}) collective-permute-start(f32[3,64,18,1]{1,2,3,0:T(8,128)} %copy.35), channel_id=1, source_target_pairs={{1,0},{2,1},{3,2},{4,3},{5,4},{6,5},{7,6},{8,7},{9,8},{10,9},{11,1... | collective-permute-start | bytes 41480 | tf_op jit(solution)/shard_map/ppermute | solution.py:30
  218.1 5.4 %collective-permute-start.12 = (f32[3,64,1,128]{3,1,2,0:T(8,128)S(1)}, f32[3,64,1,128]{3,1,2,0:T(8,128)S(1)}, u32[]{:S(2)}, u32[]{:S(2)}) collective-permute-start(f32[3,64,1,128]{3,1,2,0:T(8,128)S(1)} %copy.44), channel_id=1, source_target_pairs={{0,16},{16,32},{32,48},{48,64},{64,80},{80,96},{96,112},{1,17},{17... | collective-permute-start | bytes 294920 | tf_op jit(solution)/shard_map/ppermute | solution.py:28
  220.1 7.5 %collective-permute-start.13 = (f32[3,64,1,128]{3,1,2,0:T(8,128)S(1)}, f32[3,64,1,128]{3,1,2,0:T(8,128)S(1)}, u32[]{:S(2)}, u32[]{:S(2)}) collective-permute-start(f32[3,64,1,128]{3,1,2,0:T(8,128)S(1)} %copy.45), channel_id=1, source_target_pairs={{16,0},{32,16},{48,32},{64,48},{80,64},{96,80},{112,96},{17,1},{33... | collective-permute-start | bytes 294920 | tf_op jit(solution)/shard_map/ppermute | solution.py:30
  227.7 20.9 %copy-start.7 = (f32[3,64,16,128]{1,3,2,0:T(8,128)S(1)}, f32[3,64,16,128]{1,3,2,0:T(8,128)}, u32[]{:S(2)}) copy-start(f32[3,64,16,128]{1,3,2,0:T(8,128)} %get-tuple-element.11) | copy-start | bytes 4718596
  229.6 16.0 %collective-permute-start.14 = (f32[3,64,18,1]{1,2,3,0:T(8,128)}, f32[3,64,18,1]{1,2,3,0:T(8,128)}, u32[]{:S(2)}, u32[]{:S(2)}) collective-permute-start(f32[3,64,18,1]{1,2,3,0:T(8,128)} %copy.48), channel_id=1, source_target_pairs={{0,1},{1,2},{2,3},{3,4},{4,5},{5,6},{6,7},{7,8},{8,9},{9,10},{10,1... | collective-permute-start | bytes 41480 | tf_op jit(solution)/shard_map/ppermute | solution.py:28
  238.6 9.2 %collective-permute-start.15 = (f32[3,64,18,1]{1,2,3,0:T(8,128)}, f32[3,64,18,1]{1,2,3,0:T(8,128)}, u32[]{:S(2)}, u32[]{:S(2)}) collective-permute-start(f32[3,64,18,1]{1,2,3,0:T(8,128)} %copy.49), channel_id=1, source_target_pairs={{1,0},{2,1},{3,2},{4,3},{5,4},{6,5},{7,6},{8,7},{9,8},{10,9},{11,1... | collective-permute-start | bytes 41480 | tf_op jit(solution)/shard_map/ppermute | solution.py:30
  299.1 5.6 %collective-permute-start.16 = (f32[3,64,1,128]{3,1,2,0:T(8,128)}, f32[3,64,1,128]{3,1,2,0:T(8,128)S(1)}, u32[]{:S(2)}, u32[]{:S(2)}) collective-permute-start(f32[3,64,1,128]{3,1,2,0:T(8,128)} %copy.58), channel_id=1, source_target_pairs={{0,16},{16,32},{32,48},{48,64},{64,80},{80,96},{96,112},{1,17},{17... | collective-permute-start | bytes 294920 | tf_op jit(solution)/shard_map/ppermute | solution.py:28
  301.2 7.6 %collective-permute-start.17 = (f32[3,64,1,128]{3,1,2,0:T(8,128)S(1)}, f32[3,64,1,128]{3,1,2,0:T(8,128)}, u32[]{:S(2)}, u32[]{:S(2)}) collective-permute-start(f32[3,64,1,128]{3,1,2,0:T(8,128)S(1)} %copy.59), channel_id=1, source_target_pairs={{16,0},{32,16},{48,32},{64,48},{80,64},{96,80},{112,96},{17,1},{33... | collective-permute-start | bytes 294920 | tf_op jit(solution)/shard_map/ppermute | solution.py:30
  310.4 14.5 %collective-permute-start.18 = (f32[3,64,18,1]{1,2,3,0:T(8,128)}, f32[3,64,18,1]{1,2,3,0:T(8,128)}, u32[]{:S(2)}, u32[]{:S(2)}) collective-permute-start(f32[3,64,18,1]{1,2,3,0:T(8,128)} %copy.62), channel_id=1, source_target_pairs={{0,1},{1,2},{2,3},{3,4},{4,5},{5,6},{6,7},{7,8},{8,9},{9,10},{10,1... | collective-permute-start | bytes 41480 | tf_op jit(solution)/shard_map/ppermute | solution.py:28
  318.0 9.2 %collective-permute-start.19 = (f32[3,64,18,1]{1,2,3,0:T(8,128)}, f32[3,64,18,1]{1,2,3,0:T(8,128)}, u32[]{:S(2)}, u32[]{:S(2)}) collective-permute-start(f32[3,64,18,1]{1,2,3,0:T(8,128)} %copy.63), channel_id=1, source_target_pairs={{1,0},{2,1},{3,2},{4,3},{5,4},{6,5},{7,6},{8,7},{9,8},{10,9},{11,1... | collective-permute-start | bytes 41480 | tf_op jit(solution)/shard_map/ppermute | solution.py:30
  (25 other events, 153.1 us)

commit v2 on v1

--- a/solution.py
+++ b/solution.py
@@ -9,81 +9,16 @@
 
 SWEEPS = 4
 CAP = 24
-
-
-NEIGHBOUR_WEIGHTS = (0.0, 1.0, 0.5, 0.25)
+NZ = 64
+CX = 16
+CY = 128
+ROWS = 8
+PARTS = NZ // ROWS
+SLAB = (PARTS, ROWS, CY)
 DIAGONAL_WEIGHT = 14.5
 COUPLING = 0.25
 SOFTENED = 0.05
 
-
-def with_halo(cells, sides, width):
-    for axis, dim in sides:
-        count = lax.axis_size(axis)
-        ends = count - 1
-        head = lax.slice_in_dim(cells, 0, width, axis=dim)
-        tail = lax.slice_in_dim(cells, cells.shape[dim] - width, cells.shape[dim], axis=dim)
-        cells = jnp.concatenate(
-            [
-                lax.ppermute(tail, axis, [(i, (i + 1) % count) for i in range(ends)]),
-                cells,
-                lax.ppermute(head, axis, [((i + 1) % count, i) for i in range(ends)]),
-            ],
-            axis=dim,
-        )
-    return cells
-
-
-def operate(padded, modulus_now):
-    depth = padded.shape[1] - 2
-    breadth = padded.shape[2] - 2
-    length = padded.shape[3] - 2
-
-    def neighbour(a, b, c):
-        return padded[:, 1 + a : 1 + a + depth, 1 + b : 1 + b + breadth, 1 + c : 1 + c + length]
-
-    middle = neighbour(0, 0, 0)
-    beside_all = jnp.zeros_like(middle)
-    for a in (-1, 0, 1):
-        for b in (-1, 0, 1):
-            for c in (-1, 0, 1):
-                distance = abs(a) + abs(b) + abs(c)
-                if distance:
-                    beside_all = beside_all + NEIGHBOUR_WEIGHTS[distance] * neighbour(a, b, c)
-    unit_steps = ((1, 0, 0), (0, 1, 0), (0, 0, 1))
-    coupled = []
-    for component in range(3):
-        summed = jnp.zeros_like(middle[0])
-        for second in range(3):
-            if second != component:
-                e = unit_steps[component]
-                f = unit_steps[second]
-                plus_plus = neighbour(e[0] + f[0], e[1] + f[1], e[2] + f[2])[second]
-                plus_minus = neighbour(e[0] - f[0], e[1] - f[1], e[2] - f[2])[second]
-                minus_plus = neighbour(f[0] - e[0], f[1] - e[1], f[2] - e[2])[second]
-                minus_minus = neighbour(-e[0] - f[0], -e[1] - f[1], -e[2] - f[2])[second]
-                summed = summed + 0.25 * (plus_plus - plus_minus - minus_plus + minus_minus)
-        coupled.append(summed)
-    return modulus_now * (DIAGONAL_WEIGHT * middle - beside_all - COUPLING * jnp.stack(coupled))
-
-
-def load_from(padded_stress):
-    along_z = 0.5 * (padded_stress[2:, 1:-1, 1:-1] - padded_stress[:-2, 1:-1, 1:-1])
-    along_x = 0.5 * (padded_stress[1:-1, 2:, 1:-1] - padded_stress[1:-1, :-2, 1:-1])
-    along_y = 0.5 * (padded_stress[1:-1, 1:-1, 2:] - padded_stress[1:-1, 1:-1, :-2])
-    return jnp.stack([along_z, along_x, along_y])
-
-
-def padded_field(field):
-    extended = with_halo(field, (("gx", 2), ("gy", 3)), 1)
-    return jnp.pad(extended, ((0, 0), (1, 1), (0, 0), (0, 0)))
-
-
-def advance(step_prev, scaled, sweep, ratio_now, sigma, delta, theta):
-    if sweep == 0:
-        return (scaled / theta, ratio_now)
-    ratio_next = 1.0 / (2.0 * sigma - ratio_now)
-    return (ratio_next * ratio_now * step_prev + 2.0 * ratio_next / delta * scaled, ratio_next)
 
 MESH = pl.DeviceIdType.MESH
 
@@ -123,7 +58,9 @@
     lax.fori_loop(1, tiles, greet, 0)
 
     owner = owner_ref[...]
-    element = element_ref[...] + 1
+    given = element_ref[...]
+    depth_index = given // CX
+    element = lax.rem(given, CX) * NZ + lax.rem(depth_index, PARTS) * ROWS + depth_index // PARTS + 1
     tile_of = lax.broadcasted_iota(jnp.int32, (tiles, count), 0)
     member = jnp.where(tile_of == owner, 1.0, 0.0)
     member16 = member.astype(jnp.bfloat16)
@@ -279,37 +216,363 @@
     )(owner, element, rows)
 
 
-def local(thermal_rows, row_owner, row_element, modulus, birth, start_disp, bounds):
-    depth = modulus.shape[0]
-    breadth = modulus.shape[1]
-    length = modulus.shape[2]
-    elements = depth * breadth
-    count = thermal_rows.shape[0]
-    summed_rows = exchange(row_owner.reshape(1, count), row_element.reshape(1, count), thermal_rows, elements)
-    increment = summed_rows.reshape(depth, breadth, length)
-    stress = modulus * increment
-    lower = bounds[0]
-    upper = bounds[1]
+def lanes():
+    return lax.broadcasted_iota(jnp.int32, (ROWS, CY), 1)
+
+
+def up(slab):
+    row = lax.broadcasted_iota(jnp.int32, (ROWS, CY), 0)
+    first = jnp.where(row == ROWS - 1, 0.0, pltpu.roll(slab[0], ROWS - 1, 0))
+    return jnp.concatenate([slab[1:], first[None]], axis=0)
+
+
+def down(slab):
+    row = lax.broadcasted_iota(jnp.int32, (ROWS, CY), 0)
+    last = jnp.where(row == 0, 0.0, pltpu.roll(slab[PARTS - 1], 1, 0))
+    return jnp.concatenate([last[None], slab[:-1]], axis=0)
+
+
+def pack_ends(slab, x, packed_ref):
+    pair = lax.rem(lanes() + 1, CY) // 2
+    ends = slab[0]
+    for part in range(1, PARTS):
+        ends = jnp.where(pair == part, pltpu.roll(slab[part], 2 * part, 1), ends)
+    turn = lax.rem(x, 8)
+    ends = pltpu.roll(ends, 2 * PARTS * turn, 1)
+    packed_ref[x // 8] = jnp.where(pair // PARTS == turn, ends, packed_ref[x // 8])
+
+
+def merge_ends(from_left, from_right):
+    return jnp.where(lax.rem(lanes(), 2) == 0, pltpu.roll(from_left, 1, 1), pltpu.roll(from_right, CY - 1, 1))
+
+
+def beside(slab, ends, turn):
+    lane = lanes()
+    ends = pltpu.roll(ends, lax.rem(CY - 2 * PARTS * turn, CY), 1)
+    left, right = [], []
+    for part in range(PARTS):
+        mine = ends if part == 0 else pltpu.roll(ends, CY - 2 * part, 1)
+        left.append(jnp.where(lane == 0, mine, pltpu.roll(slab[part], 1, 1)))
+        right.append(jnp.where(lane == CY - 1, mine, pltpu.roll(slab[part], CY - 1, 1)))
+    return jnp.stack(left), jnp.stack(right)
+
+
+def sweep_kernel(
+    nx, ny, bounds_ref, increment_ref, modulus_ref, birth_ref, start_ref, out_ref,
+    fields, stress, inverse, forces, born, steps, mixed,
+    packed, packed_stress, got_ends, got_stress_ends, ends, ends_stress,
+    face_send, face_recv, side_send, side_recv, corner_send, corner_recv,
+    stress_face_send, stress_face_recv, stress_side_send, stress_side_recv,
+):
+    gx = lax.axis_index("gx")
+    gy = lax.axis_index("gy")
+    has = {-1: (gx > 0, gy > 0), 1: (gx < nx - 1, gy < ny - 1)}
+    places = [(a, b) for a in (-1, 0, 1) for b in (-1, 0, 1) if (a, b) != (0, 0)]
+
+    def present(a, b):
+        if a == 0:
+            return has[b][1]
+        if b == 0:
+            return has[a][0]
+        return jnp.logical_and(has[a][0], has[b][1])
+
+    barrier = pltpu.get_barrier_semaphore()
+    for a, b in places:
+
+        @pl.when(present(a, b))
+        def _(a=a, b=b):
+            pl.semaphore_signal(barrier, inc=1, device_id=(gx + a, gy + b), device_id_type=MESH)
+
+    zeros = jnp.zeros((ROWS, CY), jnp.float32)
+    for side, slab_at, group_at in ((-1, 0, 0), (1, CX + 1, 3)):
+
+        @pl.when(jnp.logical_not(has[side][0]))
+        def _(slab_at=slab_at, group_at=group_at):
+            stress[slab_at] = jnp.zeros(SLAB, jnp.float32)
+            for sweep in range(SWEEPS):
+                for c in range(3):
+                    fields[sweep, c, slab_at] = jnp.zeros(SLAB, jnp.float32)
+                    for hand in range(2):
+                        got_ends[sweep, hand, c, group_at] = zeros
+
+        @pl.when(jnp.logical_not(has[side][1]))
+        def _(hand=(side + 1) // 2):
+            for group in range(2):
+                got_stress_ends[hand, group] = zeros
+            for sweep in range(SWEEPS):
+                for c in range(3):
+                    for group in range(4):
+                        got_ends[sweep, hand, c, group] = zeros
+
+    def rows_of(x, part):
+        return pl.ds(part * CX + x, ROWS, stride=CX * PARTS)
+
+    def take(ref, x):
+        return jnp.stack([ref[rows_of(x, part), :] for part in range(PARTS)])
+
+    def begin(x, carry):
+        for c in range(3):
+            slab = take(start_ref.at[c], x)
+            fields[0, c, x + 1] = slab
+            pack_ends(slab, x, packed.at[0, c])
+        return carry
+
+    lax.fori_loop(0, CX, begin, 0)
+
+    def strain(x, carry):
+        modulus = take(modulus_ref, x)
+        inverse[x] = 1.0 / (DIAGONAL_WEIGHT * modulus)
+        born[x] = take(birth_ref, x)
+        slab = modulus * increment_ref[pl.ds(x * NZ, NZ), :].reshape(SLAB)
+        stress[x + 1] = slab
+        pack_ends(slab, x, packed_stress)
+        return carry
+
+    lax.fori_loop(0, CX, strain, 0)
+
+    columns = 1 + (gx + nx - 1) // nx + (2 * nx - 2 - gx) // nx
+    lines = 1 + (gy + ny - 1) // ny + (2 * ny - 2 - gy) // ny
+    pl.semaphore_wait(barrier, columns * lines - 1)
+
+    def face(sweep, a):
+        mine, theirs = (1, CX + 1) if a < 0 else (CX, 0)
+        return pltpu.make_async_remote_copy(
+            src_ref=fields.at[sweep, :, mine], dst_ref=fields.at[sweep, :, theirs],
+            send_sem=face_send.at[sweep, (a + 1) // 2], recv_sem=face_recv.at[sweep, (1 - a) // 2],
+            device_id=(gx + a, gy), device_id_type=MESH,
+        )
+
+    def side(sweep, b):
+        return pltpu.make_async_remote_copy(
+            src_ref=packed.at[sweep], dst_ref=got_ends.at[sweep, (1 - b) // 2, :, pl.ds(1, 2)],
+            send_sem=side_send.at[sweep, (b + 1) // 2], recv_sem=side_recv.at[sweep, (1 - b) // 2],
+            device_id=(gx, gy + b), device_id_type=MESH,
+        )
+
+    def corner(sweep, a, b):
+        mine, theirs = (0, 3) if a < 0 else (1, 0)
+        return pltpu.make_async_remote_copy(
+            src_ref=packed.at[sweep, :, mine], dst_ref=got_ends.at[sweep, (1 - b) // 2, :, theirs],
+            send_sem=corner_send.at[sweep, a + 1 + (b + 1) // 2], recv_sem=corner_recv.at[sweep, 1 - a + (1 - b) // 2],
+            device_id=(gx + a, gy + b), device_id_type=MESH,
+        )
+
+    def stress_face(a):
+        mine, theirs = (1, CX + 1) if a < 0 else (CX, 0)
+        return pltpu.make_async_remote_copy(
+            src_ref=stress.at[mine], dst_ref=stress.at[theirs],
+            send_sem=stress_face_send.at[(a + 1) // 2], recv_sem=stress_face_recv.at[(1 - a) // 2],
+            device_id=(gx + a, gy), device_id_type=MESH,
+        )
+
+    def stress_side(b):
+        return pltpu.make_async_remote_copy(
+            src_ref=packed_stress, dst_ref=got_stress_ends.at[(1 - b) // 2],
+            send_sem=stress_side_send.at[(b + 1) // 2], recv_sem=stress_side_recv.at[(1 - b) // 2],
+            device_id=(gx, gy + b), device_id_type=MESH,
+        )
+
+    def over(copies, do):
+        for where, copy in copies:
+
+            @pl.when(present(*where))
+            def _(copy=copy):
+                do(copy())
+
+    def faces(sweep):
+        return [((a, 0), lambda a=a: face(sweep, a)) for a in (-1, 1)]
+
+    def edges(sweep):
+        return [((0, b), lambda b=b: side(sweep, b)) for b in (-1, 1)] + [
+            ((a, b), lambda a=a, b=b: corner(sweep, a, b)) for a in (-1, 1) for b in (-1, 1)
+        ]
+
+    of_stress = [((a, 0), lambda a=a: stress_face(a)) for a in (-1, 1)] + [
+        ((0, b), lambda b=b: stress_side(b)) for b in (-1, 1)
+    ]
+
+    def arrival(ref, sem):
+        return lambda: pltpu.make_async_copy(ref, ref, sem)
+
+    def from_faces(sweep):
+        return [
+            ((a, 0), arrival(fields.at[sweep, :, 0 if a < 0 else CX + 1], face_recv.at[sweep, (a + 1) // 2])) for a in (-1, 1)
+        ]
+
+    def from_edges(sweep):
+        return [
+            ((0, b), arrival(got_ends.at[sweep, (b + 1) // 2, :, pl.ds(1, 2)], side_recv.at[sweep, (b + 1) // 2]))
+            for b in (-1, 1)
+        ] + [
+            (
+                (a, b),
+                arrival(
+                    got_ends.at[sweep, (b + 1) // 2, :, 0 if a < 0 else 3],
+                    corner_recv.at[sweep, a + 1 + (b + 1) // 2],
+                ),
+            )
+            for a in (-1, 1)
+            for b in (-1, 1)
+        ]
+
+    of_stress_arrived = [
+        ((a, 0), arrival(stress.at[0 if a < 0 else CX + 1], stress_face_recv.at[(a + 1) // 2])) for a in (-1, 1)
+    ] + [((0, b), arrival(got_stress_ends.at[(b + 1) // 2], stress_side_recv.at[(b + 1) // 2])) for b in (-1, 1)]
+
+    def start(copy):
+        copy.start()
+
+    def receive(copy):
+        copy.wait()
+
+    def finish(copy):
+        copy.wait_send()
+
+    over(of_stress, start)
+    over(edges(0), start)
+    over(faces(0), start)
+
+    lower = jnp.full((ROWS, CY), bounds_ref[0], jnp.float32)
+    upper = jnp.full((ROWS, CY), bounds_ref[1], jnp.float32)
     theta = (upper + lower) / 2.0
     delta = (upper - lower) / 2.0
     sigma = theta / delta
-    ratio_now = 1.0 / sigma
-    field = start_disp
-    step_field = jnp.zeros_like(field)
-    stress_ext = with_halo(stress, (("gx", 1), ("gy", 2)), 1)
-    load = load_from(jnp.pad(stress_ext, ((1, 1), (0, 0), (0, 0))))
-    first_padded = padded_field(field)
+    ratio = 1.0 / sigma
+
+    over(of_stress_arrived, receive)
+    for group in range(2):
+        ends_stress[group] = merge_ends(got_stress_ends[0, group], got_stress_ends[1, group])
+
+    def force(x, carry):
+        middle = stress[x + 1]
+        left, right = beside(middle, ends_stress[x // 8], lax.rem(x, 8))
+        scale = 0.5 * inverse[x]
+        forces[0, x] = scale * (up(middle) - down(middle))
+        forces[1, x] = scale * (stress[x + 2] - stress[x])
+        forces[2, x] = scale * (right - left)
+        return carry
+
+    lax.fori_loop(0, CX, force, 0)
+
     for sweep in range(SWEEPS):
-        active = modulus * jnp.where(birth <= sweep, 1.0, SOFTENED).astype(jnp.float32)
+        last = sweep == SWEEPS - 1
+        over(from_edges(sweep) + from_faces(sweep), receive)
+        for c in range(3):
+            for group in range(4):
+                ends[c, group] = merge_ends(got_ends[sweep, 0, c, group], got_ends[sweep, 1, c, group])
+
+        def along(at, carry, sweep=sweep):
+            for c in range(3):
+                slab = fields[sweep, c, at]
+                left, right = beside(slab, ends[c, (at + 7) // 8], lax.rem(at + 7, 8))
+                mixed[c, at] = (left + right) + 2.0 * slab
+                mixed[3 + c, at] = right - left
+            return carry
+
+        lax.fori_loop(0, CX + 2, along, 0)
+
         if sweep == 0:
-            padded = first_padded
+            gain = 1.0 / theta
         else:
-            padded = padded_field(field)
-        residual = load - operate(padded, active)
-        scaled = residual / (DIAGONAL_WEIGHT * active)
-        step_field, ratio_now = advance(step_field, scaled, sweep, ratio_now, sigma, delta, theta)
-        field = field + step_field
-    return field
+            ratio_next = 1.0 / (2.0 * sigma - ratio)
+            keep = ratio_next * ratio
+            gain = 2.0 * ratio_next / delta
+            ratio = ratio_next
+
+        def across(x, sweep=sweep, last=last, gain=gain, keep=None if sweep == 0 else keep):
+            at = x + 1
+            softer = jnp.where(born[x] <= sweep, 1.0, 1.0 / SOFTENED)
+            crossed = (
+                (fields[sweep, 1, at + 1] - fields[sweep, 1, at - 1]) + mixed[5, at],
+                fields[sweep, 0, at + 1] - fields[sweep, 0, at - 1],
+                mixed[3, at],
+            )
+            for c in range(3):
+                around = (mixed[c, at - 1] + mixed[c, at + 1]) + 2.0 * mixed[c, at]
+                around = (up(around) + down(around)) + 2.0 * around
+                coupled = up(crossed[c]) - down(crossed[c])
+                if c == 1:
+                    coupled = coupled + (mixed[5, at + 1] - mixed[5, at - 1])
+                if c == 2:
+                    coupled = coupled + (mixed[4, at + 1] - mixed[4, at - 1])
+                around = around + COUPLING * coupled
+                slab = fields[sweep, c, at]
+                scaled = (
+                    (0.25 / DIAGONAL_WEIGHT) * around
+                    - ((DIAGONAL_WEIGHT + 2.0) / DIAGONAL_WEIGHT) * slab
+                    + softer * forces[c, x]
+                )
+                step = gain * scaled
+                if sweep:
+                    step = step + keep * steps[c, x]
+                moved = slab + step
+                if last:
+                    for part in range(PARTS):
+                        out_ref[c, rows_of(x, part), :] = moved[part]
+                else:
+                    steps[c, x] = step
+                    fields[sweep + 1, c, at] = moved
+                    pack_ends(moved, x, packed.at[sweep + 1, c])
+
+        def across_loop(x, carry, across=across):
+            across(x)
+            return carry
+
+        if last:
+            lax.fori_loop(0, CX, across_loop, 0)
+        else:
+            lax.fori_loop(0, 2, lambda i, carry, across=across: (across(i * (CX - 1)), carry)[1], 0)
+            over(faces(sweep + 1), start)
+            lax.fori_loop(1, CX - 1, across_loop, 0)
+            over(edges(sweep + 1), start)
+
+    over(of_stress, finish)
+    for sweep in range(SWEEPS):
+        over(edges(sweep) + faces(sweep), finish)
+
+
+def sweeps(bounds, increment, modulus, birth, start_disp):
+    nx, ny = lax.axis_size("gx"), lax.axis_size("gy")
+    cells = NZ * CX
+    f32 = jnp.float32
+    vmem = pl.BlockSpec(memory_space=pltpu.VMEM)
+    dma = pltpu.SemaphoreType.DMA
+    moved = pl.pallas_call(
+        functools.partial(sweep_kernel, nx, ny),
+        out_shape=jax.ShapeDtypeStruct((3, cells, CY), f32),
+        in_specs=[pl.BlockSpec(memory_space=pltpu.SMEM)] + [vmem] * 4,
+        out_specs=vmem,
+        scratch_shapes=[
+            pltpu.VMEM((SWEEPS, 3, CX + 2) + SLAB, f32),
+            pltpu.VMEM((CX + 2,) + SLAB, f32),
+            pltpu.VMEM((CX,) + SLAB, f32),
+            pltpu.VMEM((3, CX) + SLAB, f32),
+            pltpu.VMEM((CX,) + SLAB, jnp.int32),
+            pltpu.VMEM((3, CX) + SLAB, f32),
+            pltpu.VMEM((6, CX + 2) + SLAB, f32),
+            pltpu.VMEM((SWEEPS, 3, 2, ROWS, CY), f32),
+            pltpu.VMEM((2, ROWS, CY), f32),
+            pltpu.VMEM((SWEEPS, 2, 3, 4, ROWS, CY), f32),
+            pltpu.VMEM((2, 2, ROWS, CY), f32),
+            pltpu.VMEM((3, 4, ROWS, CY), f32),
+            pltpu.VMEM((2, ROWS, CY), f32),
+            dma((SWEEPS, 2)), dma((SWEEPS, 2)), dma((SWEEPS, 2)), dma((SWEEPS, 2)), dma((SWEEPS, 4)), dma((SWEEPS, 4)),
+            dma((2,)), dma((2,)), dma((2,)), dma((2,)),
+        ],
+        compiler_params=pltpu.CompilerParams(
+            collective_id=1, has_side_effects=True, vmem_limit_bytes=40 * 1024 * 1024
+        ),
+        name="sweeps",
+    )(
+        bounds, increment, modulus.reshape(cells, CY), birth.reshape(cells, CY), start_disp.reshape(3, cells, CY)
+    )
+    return moved.reshape(start_disp.shape)
+
+
+def local(thermal_rows, row_owner, row_element, modulus, birth, start_disp, bounds):
+    count = thermal_rows.shape[0]
+    increment = exchange(row_owner.reshape(1, count), row_element.reshape(1, count), thermal_rows, NZ * CX)
+    return sweeps(bounds, increment, modulus, birth, start_disp)
 
 
 def solution(mesh):

time: 385 us -> 94.8 us (0.25); the launches traced: 379 us -> 94.4 us
  other arithmetic: 197 us -> 0 us
  starting transfers between devices: 71.9 us -> 0 us
  Pallas kernels: 35.6 us -> 88.6 us
  local copies, waits for them, and re-layouts: 48.4 us -> 5.73 us
  waiting for transfers between devices: 21.4 us -> 0 us
  between operations: 3.9 us -> 0.05 us
    add x12 -> x0, other arithmetic: 170 us -> none  [the longest x4 149 us: local(): field = field + step_field]
    ppermute x20 -> x0, starting transfers between devices: 71.9 us -> none  [the longest x10 45.8 us: with_halo(): lax.ppermute(tail, axis, [(i, (i + 1) % count) for i in range(ends)])]
    pallas_call x0 -> x1, Pallas kernels: none -> 54.4 us  [sweeps(): pl.pallas_call(functools.partial(sweep_kernel, nx, ny), out_shape=jax.Sha...]
    concatenate x14 -> x0, other arithmetic: 23 us -> none  [with_halo(): jnp.concatenate([lax.ppermute(tail, axis, [(i, (i + 1) % count) for i in...]
    ppermute x20 -> x0, waiting for transfers between devices: 21.4 us -> none  [the longest x10 21.1 us: with_halo(): lax.ppermute(head, axis, [((i + 1) % count, i) for i in range(ends)])]
    mul x7 -> x0, local copies, waits for them, and re-layouts: 17 us -> none  [the longest x4 9.95 us: local(): modulus * jnp.where(birth <= sweep, 1.0, SOFTENED).astype(jnp.float32)]
    ppermute x16 -> x0, local copies, waits for them, and re-layouts: 9.43 us -> none  [the longest x8 5.6 us: with_halo(): lax.ppermute(head, axis, [((i + 1) % count, i) for i in range(ends)])]
    slice x20 -> x0, local copies, waits for them, and re-layouts: 8.93 us -> none  [the longest x12 6.09 us: with_halo(): lax.slice_in_dim(cells, cells.shape[dim] - width, cells.shape[dim], axis=...]
  transfers between devices with their start and end apart: 20 -> 0, of which waited for: 9 -> 0; matrix products, arithmetic and copies ran while one was open for 10% -> 0% of each run, Pallas kernels for 9% -> 0%
where the time goes in v2:
time: 94.8 us; the launch traced here: 94.4 us
  Pallas kernels  88.6 us (93%)
  local copies, waits for them, and re-layouts  5.73 us (6%)
    pallas_call x1, Pallas kernels, sweeps(): pl.pallas_call(functools.partial(sweep_kernel, nx, ny), out_shape=jax.Sha...  54.4 us
    pallas_call x1, Pallas kernels, exchange(): pl.pallas_call(functools.partial(exchange_kernel, nx, ny), out_shape=jax....  34.3 us
    unnamed x15, local copies, waits for them, and re-layouts  5.73 us

profile of v2, /device:TPU:31, one launch (start us, length us, event | category | flops | bytes accessed | tf_op | source)
XLA Modules:
  0.0 94.4 jit_solution(4751875453309747243)
XLA Ops:
  0.0 0.0 copy-start.1
  0.0 1.1 %copy-done.1 = f32[1536,128]{1,0:T(8,128)S(1)} copy-done((f32[1536,128]{1,0:T(8,128)S(1)}, f32[1536,128]{1,0:T(8,128)}, u32[]{:S(2)}) %copy-start.1) | copy-done | bytes 786456
  1.1 0.0 copy-start.4
  1.1 0.7 copy-done.4
  1.8 0.0 copy-start.5
  1.8 0.7 copy-done.5
  2.5 0.0 copy-start.2
  2.5 0.0 copy-start.3
  2.5 34.3 %exchange.1.increment_ref = f32[1024,128]{1,0:T(8,128)S(1)} custom-call(s32[1,1536]{1,0:T(1,128)S(1)} %bitcast.10, s32[1,1536]{1,0:T(1,128)S(1)} %bitcast.11, f32[1536,128]{1,0:T(8,128)S(1)} %copy-done.1), custom_call_target="tpu_custom_call" | custom-call | tf_op jit(solution)/shard_map/exchange/pallas_call | solution.py:194
  36.8 0.0 copy-done.2
  36.8 0.0 copy-done.3
  36.8 0.0 copy-start
  36.8 1.4 %copy-done = f32[3,64,16,128]{3,2,1,0:T(8,128)S(1)} copy-done((f32[3,64,16,128]{3,2,1,0:T(8,128)S(1)}, f32[3,64,16,128]{3,2,1,0:T(8,128)}, u32[]{:S(2)}) %copy-start) | copy-done | bytes 1572888
  38.2 0.0 copy-start.6
  38.2 0.7 copy-done.6
  38.9 54.4 %sweeps.1 = f32[3,1024,128]{2,1,0:T(8,128)S(1)} custom-call(f32[2]{0:T(128)S(1)} %copy-done.6, f32[1024,128]{1,0:T(8,128)S(1)} %exchange.1.increment_ref, f32[1024,128]{1,0:T(8,128)S(1)} %bitcast.8, s32[1024,128]{1,0:T(8,128)S(1)} %bitcast.9, f32[3,1024,128]{2,1,0:T(8,128)S(1)} %bitcast.7), custom_call_target="tpu_custom_call" | custom-call | tf_op jit(solution)/shard_map/sweeps/pallas_call | solution.py:540
  93.2 1.1 %copy.9 = f32[3,64,16,128]{3,2,1,0:T(8,128)} copy(f32[3,64,16,128]{3,2,1,0:T(8,128)S(1)} %bitcast.6) | data formatting | bytes 3145728
Async XLA Ops:
  0.0 1.1 %copy-start.1 = (f32[1536,128]{1,0:T(8,128)S(1)}, f32[1536,128]{1,0:T(8,128)}, u32[]{:S(2)}) copy-start(f32[1536,128]{1,0:T(8,128)} %rows_ref.1) | copy-start | bytes 2359300
  1.1 0.7 copy-start.4
  1.8 0.7 copy-start.5
  2.5 34.3 %copy-start.2 = (f32[64,16,128]{2,1,0:T(8,128)S(1)}, f32[64,16,128]{2,1,0:T(8,128)}, u32[]{:S(2)}) copy-start(f32[64,16,128]{2,1,0:T(8,128)} %param.10) | copy-start | bytes 1572868
  2.5 34.3 %copy-start.3 = (s32[64,16,128]{2,1,0:T(8,128)S(1)}, s32[64,16,128]{2,1,0:T(8,128)}, u32[]{:S(2)}) copy-start(s32[64,16,128]{2,1,0:T(8,128)} %param.11) | copy-start | bytes 1572868
  36.8 1.4 %copy-start = (f32[3,64,16,128]{3,2,1,0:T(8,128)S(1)}, f32[3,64,16,128]{3,2,1,0:T(8,128)}, u32[]{:S(2)}) copy-start(f32[3,64,16,128]{3,2,1,0:T(8,128)} %param.12) | copy-start | bytes 4718596
  38.2 0.7 copy-start.6

commit v3 on v0

v3 whole, which is shorter than its diff:
```python
import functools

import jax
import jax.numpy as jnp
from jax import lax
from jax.experimental import pallas as pl
from jax.experimental.pallas import tpu as pltpu
from jax.sharding import PartitionSpec as P

SWEEPS = 4
CAP = 24
NZ = 64
CX = 16
CY = 128
ROWS = 8
PARTS = 8
HALF = CY // 2
CELLS = NZ * CX
SLABS = CX + 2
SLAB = (PARTS, ROWS, CY)
DIAGONAL_WEIGHT = 14.5
COUPLING = 0.25
SOFTENED = 0.05

MESH = pl.DeviceIdType.MESH
F32 = jnp.float32
BF16 = jnp.bfloat16


def halves(values):
    high = values.astype(BF16)
    low = (values - high.astype(F32)).astype(BF16)
    return high, low


def onehot(matches):
    return jnp.where(matches, 1.0, 0.0).astype(BF16)


def iota(shape, dim):
    return lax.broadcasted_iota(jnp.int32, shape, dim)


def product(left, right):
    return jnp.dot(left, right, preferred_element_type=F32)


def row_index():
    return iota((ROWS, CY), 0)


def in_first_half():
    return iota((ROWS, CY), 1) < HALF


def up(slab, ends):
    first = pltpu.roll(slab[0], ROWS - 1, 0)
    turned = jnp.where(in_first_half(), pltpu.roll(first, HALF, 1), ends)
    return jnp.concatenate([slab[1:], jnp.where(row_index() == ROWS - 1, turned, first)[None]], axis=0)


def down(slab, ends):
    last = pltpu.roll(slab[PARTS - 1], 1, 0)
    turned = jnp.where(in_first_half(), ends, pltpu.roll(last, HALF, 1))
    return jnp.concatenate([jnp.where(row_index() == 0, turned, last)[None], slab[:-1]], axis=0)


def end_row(slab):
    return jnp.where(iota((1, CY), 1) < HALF, slab[0][:1], pltpu.roll(slab[PARTS - 1], 1, 0)[:1])


def turn_halves(values):
    return pltpu.roll(values, HALF, 1)


def kernel(
    nx, ny,
    owner_hbm, element_hbm, rows_hbm, modulus_hbm, birth_hbm, start_hbm, bounds_ref,
    out_ref,
    owner_ref, element_ref, rows_ref, modulus_ref, birth_ref, start_ref, in_sem,
    split_ref, place_ref, send_rows, send_ids, got_rows, got_ids, total,
    ids_send_sem, ids_recv_sem, rows_send_sem, rows_recv_sem,
    fields, stress, inverse, forces, born, steps, summed, differed, sliced,
    along_matrix, turning,
    packed, packed_stress, got_ends, got_stress_ends, ends, ends_summed, ends_differed, ends_added,
    face_send, face_recv, side_send, side_recv, corner_send, corner_recv,
    stress_face_send, stress_face_recv, stress_side_send, stress_side_recv,
):
    tiles = nx * ny
    count = rows_ref.shape[0]
    group = ny * CAP
    gx = lax.axis_index("gx")
    gy = lax.axis_index("gy")

    loads = [
        pltpu.make_async_copy(source, target, in_sem.at[i])
        for i, (source, target) in enumerate(
            [
                (owner_hbm, owner_ref), (element_hbm, element_ref), (rows_hbm, rows_ref),
                (start_hbm, start_ref), (modulus_hbm, modulus_ref), (birth_hbm, birth_ref),
            ]
        )
    ]
    for load in loads:
        load.start()

    def there(step):
        return lax.rem(gx + step // ny, nx), lax.rem(gy + lax.rem(step, ny), ny)

    def number(device):
        return device[0] * ny + device[1]

    barrier = pltpu.get_barrier_semaphore()

    def greet(step, carry):
        pl.semaphore_signal(barrier, inc=1, device_id=there(step), device_id_type=MESH)
        return carry

    lax.fori_loop(1, tiles, greet, 0)

    has = {-1: (gx > 0, gy > 0), 1: (gx < nx - 1, gy < ny - 1)}

    def present(a, b):
        if a == 0:
            return has[b][1]
        if b == 0:
            return has[a][0]
        return jnp.logical_and(has[a][0], has[b][1])

    def over(copies, do):
        for where, copy in copies:

            @pl.when(present(*where))
            def _(copy=copy):
                do(copy())

    loads[0].wait()
    loads[1].wait()
    owner = owner_ref[...]
    given = element_ref[...]
    depth_index = given // CX
    element = lax.rem(given, CX) * NZ + depth_index + 1
    member = jnp.where(iota((tiles, count), 0) == owner, 1.0, 0.0)
    member16 = member.astype(BF16)
    block = 256
    earlier = onehot(iota((block, block), 0) < iota((block, block), 1))
    carried = jnp.zeros((tiles, 1), F32)
    slots = []
    for first in range(0, count, block):
        part = member[:, first : first + block]
        before = product(member16[:, first : first + block], earlier) + carried
        slots.append(jnp.sum(before * part, axis=0, keepdims=True))
        carried = carried + jnp.sum(part, axis=1, keepdims=True)
    slot = jnp.concatenate(slots, axis=1).astype(jnp.int32)
    place_ref[...] = owner * CAP + slot

    weighed = jnp.concatenate(
        [
            (member * (element // 32).astype(F32)).astype(BF16),
            (member * lax.rem(element, 32).astype(F32)).astype(BF16),
        ],
        axis=0,
    )
    slot_of = onehot(iota((CY, count), 0) == slot)
    both = lax.dot_general(weighed, slot_of, (((1,), (1,)), ((), ())), preferred_element_type=F32)
    send_ids[...] = (32.0 * both[:tiles] + both[tiles:]).reshape(tiles, 1, CY)

    loads[2].wait()
    high, low = halves(rows_ref[...])
    split_ref[:, :CY] = high
    split_ref[:, CY:] = low

    pl.semaphore_wait(barrier, tiles - 1)

    def send_id(step, carry):
        to = there(step)
        pltpu.make_async_remote_copy(
            src_ref=send_ids.at[number(to)], dst_ref=got_ids.at[step],
            send_sem=ids_send_sem, recv_sem=ids_recv_sem,
            device_id=to, device_id_type=MESH,
        ).start()
        return carry

    lax.fori_loop(1, tiles, send_id, 0)
    got_ids[0] = send_ids[number((gx, gy))]

    def pack_rows(turn, carry):
        tile_x = lax.rem(gx + turn, nx)
        wanted = tile_x * group + iota((group, count), 0)
        picked = product(onehot(wanted == place_ref[...]), split_ref[...])
        send_rows[pl.ds(tile_x * ny, ny)] = (picked[:, :CY] + picked[:, CY:]).reshape(ny, CAP, CY)

        def send(turn_y, carry):
            tile_y = lax.rem(gy + turn_y, ny)
            pltpu.make_async_remote_copy(
                src_ref=send_rows.at[tile_x * ny + tile_y], dst_ref=got_rows.at[turn * ny + turn_y],
                send_sem=rows_send_sem, recv_sem=rows_recv_sem.at[turn],
                device_id=(tile_x, tile_y), device_id_type=MESH,
            ).start()
            return carry

        @pl.when(turn == 0)
        def _():
            lax.fori_loop(1, ny, send, 0)

        @pl.when(turn > 0)
        def _():
            lax.fori_loop(0, ny, send, 0)

        return carry

    lax.fori_loop(0, nx, pack_rows, 0)
    got_rows[0] = send_rows[number((gx, gy))]

    zeros = jnp.zeros((ROWS, CY), F32)
    for hand, slab_at, group_at in ((-1, 0, 0), (1, CX + 1, 3)):

        @pl.when(jnp.logical_not(has[hand][0]))
        def _(slab_at=slab_at, group_at=group_at):
            stress[slab_at] = jnp.zeros(SLAB, F32)
            for sweep in range(SWEEPS):
                for c in range(3):
                    fields[sweep, c, slab_at] = jnp.zeros(SLAB, F32)
                    for side_at in range(2):
                        got_ends[sweep, side_at, c, group_at] = zeros

        @pl.when(jnp.logical_not(has[hand][1]))
        def _(side_at=(hand + 1) // 2):
            got_stress_ends[side_at] = jnp.zeros((2, ROWS, CY), F32)
            for sweep in range(SWEEPS):
                for c in range(3):
                    got_ends[sweep, side_at, c] = jnp.zeros((4, ROWS, CY), F32)

    row, column = iota((2 * CY, 2 * CY), 0), iota((2 * CY, 2 * CY), 1)
    k, z = lax.rem(row, CY), lax.rem(column, CY)
    off = jnp.where(k // NZ == z // NZ, k - z, 2)
    after, before = jnp.where(off == 1, 1.0, 0.0), jnp.where(off == -1, 1.0, 0.0)
    sums = jnp.where(off == 0, 2.0, after + before)
    along_matrix[...] = jnp.where(column < CY, sums, after - before).astype(BF16)

    first_half = iota((2 * NZ // 2, CY), 1) < HALF

    def slabs_of(pair, at):
        turned = pair.T
        begin, end = turned[:NZ], turned[NZ:]
        slabs = []
        for odd, values in enumerate(
            (jnp.where(first_half, begin, turn_halves(end)), jnp.where(first_half, turn_halves(begin), end))
        ):
            turning[2 * at + odd] = values
            slabs.append(jnp.stack([turning[2 * at + odd, pl.ds(part, ROWS, stride=PARTS), :] for part in range(PARTS)]))
        return slabs

    def pair_of_slabs(slabs, at):
        for odd in range(2):
            for part in range(PARTS):
                turning[2 * at + odd, pl.ds(part, ROWS, stride=PARTS), :] = slabs[odd][part]
        even, odd = turning[2 * at], turning[2 * at + 1]
        return jnp.concatenate(
            [jnp.where(first_half, even, turn_halves(odd)), jnp.where(first_half, turn_halves(even), odd)], axis=0
        ).T

    def rows_of(x, part):
        return pl.ds(part * ROWS * CX + x, ROWS, stride=CX)

    def take(ref, i):
        return jnp.concatenate([ref[rows_of(2 * i + odd, part), :] for odd in range(2) for part in range(NZ // ROWS)], axis=0)

    def slice_up(slab, at):
        high, low = halves(slab.reshape(NZ, CY))
        sliced[at, :, :CY] = high
        sliced[at, :, CY:] = low

    def merge_ends(from_left, from_right):
        return turn_halves(jnp.where(in_first_half(), from_right, from_left))

    def face(sweep, a):
        mine, theirs = (1, CX + 1) if a < 0 else (CX, 0)
        return pltpu.make_async_remote_copy(
            src_ref=fields.at[sweep, :, mine], dst_ref=fields.at[sweep, :, theirs],
            send_sem=face_send.at[sweep, (a + 1) // 2], recv_sem=face_recv.at[sweep, (1 - a) // 2],
            device_id=(gx + a, gy), device_id_type=MESH,
        )

    def side(sweep, b):
        return pltpu.make_async_remote_copy(
            src_ref=packed.at[sweep], dst_ref=got_ends.at[sweep, (1 - b) // 2, :, pl.ds(1, 2)],
            send_sem=side_send.at[sweep, (b + 1) // 2], recv_sem=side_recv.at[sweep, (1 - b) // 2],
            device_id=(gx, gy + b), device_id_type=MESH,
        )

    def corner(sweep, a, b):
        mine, theirs = (0, 3) if a < 0 else (1, 0)
        return pltpu.make_async_remote_copy(
            src_ref=packed.at[sweep, :, mine], dst_ref=got_ends.at[sweep, (1 - b) // 2, :, theirs],
            send_sem=corner_send.at[sweep, a + 1 + (b + 1) // 2], recv_sem=corner_recv.at[sweep, 1 - a + (1 - b) // 2],
            device_id=(gx + a, gy + b), device_id_type=MESH,
        )

    def stress_face(a):
        mine, theirs = (1, CX + 1) if a < 0 else (CX, 0)
        return pltpu.make_async_remote_copy(
            src_ref=stress.at[mine], dst_ref=stress.at[theirs],
            send_sem=stress_face_send.at[(a + 1) // 2], recv_sem=stress_face_recv.at[(1 - a) // 2],
            device_id=(gx + a, gy), device_id_type=MESH,
        )

    def stress_side(b):
        return pltpu.make_async_remote_copy(
            src_ref=packed_stress, dst_ref=got_stress_ends.at[(1 - b) // 2],
            send_sem=stress_side_send.at[(b + 1) // 2], recv_sem=stress_side_recv.at[(1 - b) // 2],
            device_id=(gx, gy + b), device_id_type=MESH,
        )

    pair_of = (-1, 1)

    def faces(sweep):
        return [((a, 0), lambda a=a: face(sweep, a)) for a in pair_of]

    def edges(sweep):
        return [((0, b), lambda b=b: side(sweep, b)) for b in pair_of] + [
            ((a, b), lambda a=a, b=b: corner(sweep, a, b)) for a in pair_of for b in pair_of
        ]

    stress_faces = [((a, 0), lambda a=a: stress_face(a)) for a in pair_of]
    stress_sides = [((0, b), lambda b=b: stress_side(b)) for b in pair_of]

    def arrival(ref, sem):
        return lambda: pltpu.make_async_copy(ref, ref, sem)

    def from_faces(sweep):
        return [
            ((a, 0), arrival(fields.at[sweep, :, 0 if a < 0 else CX + 1], face_recv.at[sweep, (a + 1) // 2]))
            for a in pair_of
        ]

    def from_edges(sweep):
        return [
            ((0, b), arrival(got_ends.at[sweep, (b + 1) // 2, :, pl.ds(1, 2)], side_recv.at[sweep, (b + 1) // 2]))
            for b in pair_of
        ] + [
            (
                (a, b),
                arrival(
                    got_ends.at[sweep, (b + 1) // 2, :, 0 if a < 0 else 3],
                    corner_recv.at[sweep, a + 1 + (b + 1) // 2],
                ),
            )
            for a in pair_of
            for b in pair_of
        ]

    from_stress_faces = [
        ((a, 0), arrival(stress.at[0 if a < 0 else CX + 1], stress_face_recv.at[(a + 1) // 2])) for a in pair_of
    ]
    from_stress_sides = [
        ((0, b), arrival(got_stress_ends.at[(b + 1) // 2], stress_side_recv.at[(b + 1) // 2])) for b in pair_of
    ]

    def start(copy):
        copy.start()

    def receive(copy):
        copy.wait()

    def finish(copy):
        copy.wait_send()

    def along_own(sweep):
        for c in range(3):
            at = pl.ds(c * SLABS + 1, CX)
            both = product(sliced[at].reshape(CX * NZ, 2 * CY), along_matrix[...])
            summed[at] = both[:, :CY].reshape((CX,) + SLAB)
            differed[at] = both[:, CY:].reshape((CX,) + SLAB)

    def along_halo(sweep):
        over(from_edges(sweep) + from_faces(sweep), receive)
        for c in range(3):
            for g in range(4):
                at = pl.ds(g * ROWS, ROWS)
                ends[c, at] = merge_ends(got_ends[sweep, 0, c, g], got_ends[sweep, 1, c, g])
        halo = [fields[sweep, c, at].reshape(NZ, CY) for c in range(3) for at in (0, CX + 1)]
        high, low = halves(jnp.concatenate(halo + [ends[c] for c in range(3)], axis=0))
        both = product(jnp.concatenate([high, low], axis=1), along_matrix[...])
        for c in range(3):
            for hand, at in enumerate((0, CX + 1)):
                first = (2 * c + hand) * NZ
                summed[c * SLABS + at] = both[first : first + NZ, :CY].reshape(SLAB)
                differed[c * SLABS + at] = both[first : first + NZ, CY:].reshape(SLAB)
            first = 6 * NZ + c * 4 * ROWS
            ends_summed[c] = both[first : first + 4 * ROWS, :CY]
            ends_differed[c] = both[first : first + 4 * ROWS, CY:]

        def near(ref, c, step):
            return ref[c, pl.ds(ROWS + step, CX), :]

        for c in range(3):
            around = (near(ends_summed, c, -1) + near(ends_summed, c, 1)) + 2.0 * near(ends_summed, c, 0)
            if c == 0:
                across = near(ends_differed, 2, 0)
            elif c == 1:
                across = near(ends, 2, 1) - near(ends, 2, -1)
            else:
                across = near(ends_differed, 0, 0) + (near(ends, 1, 1) - near(ends, 1, -1))
            sign = jnp.where(iota((CX, CY), 1) < HALF, -COUPLING, COUPLING)
            ends_added[c] = around + sign * across

    def rest(sweep, x, c):
        at = x + 1

        def field(component, to):
            return fields[sweep, component, to]

        def along_sum(to):
            return summed[c * SLABS + to]

        def along_difference(component, to):
            return differed[component * SLABS + to]

        around = (along_sum(at - 1) + along_sum(at + 1)) + 2.0 * along_sum(at)
        if c == 0:
            across = along_difference(2, at)
        elif c == 1:
            across = field(2, at + 1) - field(2, at - 1)
        else:
            across = along_difference(0, at) + (field(1, at + 1) - field(1, at - 1))
        across = COUPLING * across
        added = ends_added[c, pl.ds(x, 1), :]
        total_around = (up(around + across, added) + down(around - across, added)) + 2.0 * around
        if c < 2:
            total_around = total_around + COUPLING * (along_difference(1 - c, at + 1) - along_difference(1 - c, at - 1))
        return (0.25 / DIAGONAL_WEIGHT) * total_around - ((DIAGONAL_WEIGHT + 2.0) / DIAGONAL_WEIGHT) * field(c, at)

    loads[3].wait()

    def store_ends(slab, x, ref):
        ref[x // ROWS, pl.ds(lax.rem(x, ROWS), 1), :] = end_row(slab)

    def begin(i, carry):
        for c in range(3):
            for odd, slab in enumerate(slabs_of(take(start_ref.at[c], i), c)):
                x = 2 * i + odd
                fields[0, c, x + 1] = slab
                slice_up(slab, c * SLABS + x + 1)
                store_ends(slab, x, packed.at[0, c])
        return carry

    lax.fori_loop(0, CX // 2, begin, 0)
    over(faces(0), start)
    over(edges(0), start)

    loads[4].wait()
    loads[5].wait()

    def material(i, carry):
        for odd, modulus in enumerate(slabs_of(take(modulus_ref, i), 0)):
            x = 2 * i + odd
            stress[x + 1] = modulus
            inverse[x] = 1.0 / (DIAGONAL_WEIGHT * modulus)
        for odd, birth in enumerate(slabs_of(take(birth_ref, i).astype(F32), 1)):
            born[2 * i + odd] = birth
        return carry

    lax.fori_loop(0, CX // 2, material, 0)
    along_own(0)

    lower = jnp.full((ROWS, CY), bounds_ref[0], F32)
    upper = jnp.full((ROWS, CY), bounds_ref[1], F32)
    theta = (upper + lower) / 2.0
    delta = (upper - lower) / 2.0
    sigma = theta / delta
    ratio = 1.0 / sigma

    along_halo(0)

    def first_rest(x, carry):
        for c in range(3):
            steps[c, x] = rest(0, x, c)
        return carry

    lax.fori_loop(0, CX, first_rest, 0, unroll=2)

    others = pl.ds(1, tiles - 1)
    pltpu.make_async_copy(got_ids.at[others], got_ids.at[others], ids_recv_sem).wait()
    spread = onehot(iota((CY, group), 0) == lax.rem(iota((CY, group), 1), CAP))
    own_lane = iota((ny, group), 0) == iota((ny, group), 1) // CAP
    total[...] = jnp.zeros_like(total)

    def collect(turn, carry):
        @pl.when(turn == 0)
        def _():
            part = got_rows.at[pl.ds(1, ny - 1)]
            pltpu.make_async_copy(part, part, rows_recv_sem.at[0]).wait()

        @pl.when(turn > 0)
        def _():
            part = got_rows.at[pl.ds(turn * ny, ny)]
            pltpu.make_async_copy(part, part, rows_recv_sem.at[turn]).wait()

        ids = got_ids[pl.ds(turn * ny, ny)].reshape(ny, CY)
        ids_high = jnp.floor(ids * (1.0 / 32.0))
        ids_low = ids - 32.0 * ids_high
        wide = 32.0 * product(ids_high.astype(BF16), spread) + product(ids_low.astype(BF16), spread)
        flat = jnp.sum(jnp.where(own_lane, wide, 0.0), axis=0, keepdims=True).astype(jnp.int32) - 1
        place = onehot(iota((CELLS, group), 0) == flat)
        high, low = halves(got_rows[pl.ds(turn * ny, ny)].reshape(group, CY))
        total[...] += product(place, jnp.concatenate([high, low], axis=1))
        return carry

    lax.fori_loop(0, nx, collect, 0)

    def strain(i, carry):
        at = pl.ds(2 * i * NZ, 2 * NZ)
        for odd, slab in enumerate(slabs_of(total[at, :CY] + total[at, CY:], 0)):
            x = 2 * i + odd
            slab = stress[x + 1] * slab
            stress[x + 1] = slab
            slice_up(slab, x + 1)
            store_ends(slab, x, packed_stress)
        return carry

    lax.fori_loop(0, CX // 2, strain, 0)
    over(stress_faces, start)
    over(stress_sides, start)
    at = pl.ds(1, CX)
    differed[at] = product(sliced[at].reshape(CX * NZ, 2 * CY), along_matrix[:, CY:]).reshape((CX,) + SLAB)
    over(from_stress_sides, receive)
    for g in range(2):
        ends[0, pl.ds(g * ROWS, ROWS)] = merge_ends(got_stress_ends[0, g], got_stress_ends[1, g])
    over(from_stress_faces, receive)

    def keep_moved(sweep, x, c, moved, step):
        at = x + 1
        steps[c, x] = step
        fields[sweep + 1, c, at] = moved
        slice_up(moved, c * SLABS + at)
        store_ends(moved, x, packed.at[sweep + 1, c])

    def softer(sweep, x):
        return jnp.where(born[x] <= sweep, 1.0, 1.0 / SOFTENED)

    first_gain = 1.0 / theta

    def first_move(x):
        middle = stress[x + 1]
        scale = 0.5 * inverse[x]
        soft = softer(0, x)
        added = ends[0, pl.ds(x, 1), :]
        gradients = (differed[x + 1], stress[x + 2] - stress[x], up(middle, added) - down(middle, added))
        for c, gradient in enumerate(gradients):
            force = scale * gradient
            forces[c, x] = force
            step = first_gain * (steps[c, x] + soft * force)
            keep_moved(0, x, c, fields[0, c, x + 1] + step, step)

    def ends_first(move, sweep):
        lax.fori_loop(0, 2, lambda i, carry: (move(i * (CX - 1)), carry)[1], 0, unroll=2)
        over(faces(sweep + 1), start)
        lax.fori_loop(1, CX - 1, lambda x, carry: (move(x), carry)[1], 0, unroll=2)
        over(edges(sweep + 1), start)
        along_own(sweep + 1)

    ends_first(first_move, 0)

    for sweep in range(1, SWEEPS):
        ratio_next = 1.0 / (2.0 * sigma - ratio)
        keep = ratio_next * ratio
        gain = 2.0 * ratio_next / delta
        ratio = ratio_next
        along_halo(sweep)

        def moves(x, sweep=sweep, keep=keep, gain=gain):
            soft = softer(sweep, x)
            for c in range(3):
                step = gain * (rest(sweep, x, c) + soft * forces[c, x]) + keep * steps[c, x]
                yield c, fields[sweep, c, x + 1] + step, step

        if sweep < SWEEPS - 1:

            def move(x, sweep=sweep, moves=moves):
                for c, moved, step in moves(x):
                    keep_moved(sweep, x, c, moved, step)

            ends_first(move, sweep)
        else:

            def last(i, carry, moves=moves):
                both = [[moved for _, moved, _ in moves(2 * i + odd)] for odd in range(2)]
                for c in range(3):
                    block = pair_of_slabs([both[0][c], both[1][c]], c)
                    for odd in range(2):
                        for part in range(NZ // ROWS):
                            first = odd * NZ + part * ROWS
                            out_ref[c, rows_of(2 * i + odd, part), :] = block[first : first + ROWS]
                return carry

            lax.fori_loop(0, CX // 2, last, 0)

    pltpu.make_async_copy(send_ids.at[others], send_ids.at[others], ids_send_sem).wait()
    pltpu.make_async_copy(send_rows.at[others], send_rows.at[others], rows_send_sem).wait()
    over(stress_faces + stress_sides, finish)
    for sweep in range(SWEEPS):
        over(edges(sweep) + faces(sweep), finish)


def local(thermal_rows, row_owner, row_element, modulus, birth, start_disp, bounds):
    nx, ny = lax.axis_size("gx"), lax.axis_size("gy")
    tiles = nx * ny
    count = thermal_rows.shape[0]
    vmem, dma = pltpu.VMEM, pltpu.SemaphoreType.DMA
    moved = pl.pallas_call(
        functools.partial(kernel, nx, ny),
        out_shape=jax.ShapeDtypeStruct((3, CELLS, CY), F32),
        in_specs=[pl.BlockSpec(memory_space=pl.ANY)] * 6 + [pl.BlockSpec(memory_space=pltpu.SMEM)],
        out_specs=pl.BlockSpec(memory_space=pltpu.VMEM),
        scratch_shapes=[
            vmem((1, count), jnp.int32),
            vmem((1, count), jnp.int32),
            vmem((count, CY), F32),
            vmem((CELLS, CY), F32),
            vmem((CELLS, CY), jnp.int32),
            vmem((3, CELLS, CY), F32),
            dma((6,)),
            vmem((count, 2 * CY), BF16),
            vmem((1, count), jnp.int32),
            vmem((tiles, CAP, CY), F32),
            vmem((tiles, 1, CY), F32),
            vmem((tiles, CAP, CY), F32),
            vmem((tiles, 1, CY), F32),
            vmem((CELLS, 2 * CY), F32),
            dma, dma, dma, dma((nx,)),
            vmem((SWEEPS, 3, SLABS) + SLAB, F32),
            vmem((SLABS,) + SLAB, F32),
            vmem((CX,) + SLAB, F32),
            vmem((3, CX) + SLAB, F32),
            vmem((CX,) + SLAB, F32),
            vmem((3, CX) + SLAB, F32),
            vmem((3 * SLABS,) + SLAB, F32),
            vmem((3 * SLABS,) + SLAB, F32),
            vmem((3 * SLABS, NZ, 2 * CY), BF16),
            vmem((2 * CY, 2 * CY), BF16),
            vmem((6, NZ, CY), F32),
            vmem((SWEEPS, 3, 2, ROWS, CY), F32),
            vmem((2, ROWS, CY), F32),
            vmem((SWEEPS, 2, 3, 4, ROWS, CY), F32),
            vmem((2, 2, ROWS, CY), F32),
            vmem((3, 4 * ROWS, CY), F32),
            vmem((3, 4 * ROWS, CY), F32),
            vmem((3, 4 * ROWS, CY), F32),
            vmem((3, CX, CY), F32),
            dma((SWEEPS, 2)), dma((SWEEPS, 2)), dma((SWEEPS, 2)), dma((SWEEPS, 2)), dma((SWEEPS, 4)), dma((SWEEPS, 4)),
            dma((2,)), dma((2,)), dma((2,)), dma((2,)),
        ],
        compiler_params=pltpu.CompilerParams(
            collective_id=0, has_side_effects=True, vmem_limit_bytes=48 * 1024 * 1024
        ),
        name="weld",
    )(
        row_owner.reshape(1, count), row_element.reshape(1, count), thermal_rows,
        modulus.reshape(CELLS, CY), birth.reshape(CELLS, CY), start_disp.reshape(3, CELLS, CY), bounds,
    )
    return moved.reshape(start_disp.shape)


def solution(mesh):
    placed = (
        P(("gx", "gy"), None),
        P(("gx", "gy"), None),
        P(("gx", "gy"), None),
        P(None, "gx", "gy"),
        P(None, "gx", "gy"),
        P(None, None, "gx", "gy"),
        P(),
    )
    return jax.shard_map(
        local, mesh=mesh, in_specs=placed, out_specs=P(None, None, "gx", "gy"), check_vma=False
    )
```

time: 359 us -> 80.4 us (0.22); the launches traced: 352 us -> 79.8 us
  other arithmetic: 159 us -> 0 us
  starting transfers between devices: 91.4 us -> 0 us
  Pallas kernels: 0 us -> 71.9 us
  local copies, waits for them, and re-layouts: 72 us -> 7.8 us
  waiting for transfers between devices: 26.1 us -> 0 us
  between operations: 3.81 us -> 0.02 us
    add x16 -> x0, other arithmetic: 84.1 us -> none  [the longest x4 49.9 us: local(): field = field + step_field]
    pallas_call x0 -> x1, Pallas kernels: none -> 71.9 us  [local(): pl.pallas_call(functools.partial(kernel, nx, ny), out_shape=jax.ShapeDtyp...]
    ppermute x20 -> x0, starting transfers between devices: 70.5 us -> none  [the longest x10 45.7 us: with_halo(): lax.ppermute(tail, axis, [(i, (i + 1) % count) for i in range(ends)])]
    concatenate x14 -> x0, other arithmetic: 49.3 us -> none  [with_halo(): jnp.concatenate([lax.ppermute(tail, axis, [(i, (i + 1) % count) for i in...]
    slice x22 -> x0, local copies, waits for them, and re-layouts: 36.4 us -> none  [the longest x10 22.4 us: with_halo(): head = lax.slice_in_dim(cells, 0, width, axis=dim)]
    ppermute x20 -> x0, waiting for transfers between devices: 26.1 us -> none  [the longest x10 26.1 us: with_halo(): lax.ppermute(head, axis, [((i + 1) % count, i) for i in range(ends)])]
    all_to_all x2 -> x0, starting transfers between devices: 20.9 us -> none  [the longest x1 11.1 us: local(): lax.all_to_all(send_ids, ('gx', 'gy'), split_axis=0, concat_axis=0, tiled...]
    ppermute x10 -> x0, local copies, waits for them, and re-layouts: 19.6 us -> none  [the longest x5 9.88 us: with_halo(): lax.ppermute(head, axis, [((i + 1) % count, i) for i in range(ends)])]
  transfers between devices with their start and end apart: 22 -> 0, of which waited for: 7 -> 0; matrix products, arithmetic and copies ran while one was open for 21% -> 0% of each run, Pallas kernels for 0% -> 0%
where the time goes in v3:
time: 80.4 us; the launch traced here: 79.8 us
  Pallas kernels  71.9 us (89%)
  local copies, waits for them, and re-layouts  7.8 us (10%)
    pallas_call x1, Pallas kernels, local(): pl.pallas_call(functools.partial(kernel, nx, ny), out_shape=jax.ShapeDtyp...  71.9 us
    unnamed x15, local copies, waits for them, and re-layouts  7.8 us

profile of v3, /device:TPU:31, one launch (start us, length us, event | category | flops | bytes accessed | tf_op | source)
XLA Modules:
  0.0 79.8 jit_solution(4582563893240180745)
XLA Ops:
  0.0 0.0 copy-start
  0.0 1.4 %copy-done = f32[3,64,16,128]{3,2,1,0:T(8,128)S(1)} copy-done((f32[3,64,16,128]{3,2,1,0:T(8,128)S(1)}, f32[3,64,16,128]{3,2,1,0:T(8,128)}, u32[]{:S(2)}) %copy-start) | copy-done | bytes 1572888
  1.4 0.0 copy-start.1
  1.4 1.1 %copy-done.1 = f32[1536,128]{1,0:T(8,128)S(1)} copy-done((f32[1536,128]{1,0:T(8,128)S(1)}, f32[1536,128]{1,0:T(8,128)}, u32[]{:S(2)}) %copy-start.1) | copy-done | bytes 786456
  2.5 0.0 copy-start.2
  2.5 1.0 %copy-done.2 = f32[64,16,128]{2,1,0:T(8,128)S(1)} copy-done((f32[64,16,128]{2,1,0:T(8,128)S(1)}, f32[64,16,128]{2,1,0:T(8,128)}, u32[]{:S(2)}) %copy-start.2) | copy-done | bytes 524312
  3.6 0.0 copy-start.3
  3.6 1.0 %copy-done.3 = s32[64,16,128]{2,1,0:T(8,128)S(1)} copy-done((s32[64,16,128]{2,1,0:T(8,128)S(1)}, s32[64,16,128]{2,1,0:T(8,128)}, u32[]{:S(2)}) %copy-start.3) | copy-done | bytes 524312
  4.6 0.0 copy-start.4
  4.6 0.7 copy-done.4
  5.3 0.0 copy-start.5
  5.3 0.7 copy-done.5
  6.0 0.0 copy-start.6
  6.0 0.7 copy-done.6
  6.7 71.9 %weld.1 = f32[3,1024,128]{2,1,0:T(8,128)S(1)} custom-call(s32[1,1536]{1,0:T(1,128)S(1)} %bitcast.10, s32[1,1536]{1,0:T(1,128)S(1)} %bitcast.11, f32[1536,128]{1,0:T(8,128)S(1)} %copy-done.1, f32[1024,128]{1,0:T(8,128)S(1)} %bitcast.8, s32[1024,128]{1,0:T(8,128)S(1)} %bitcast.9, f32[3,1024,128]{2,1,0:T(8,128)S(1)} %bitcast.7, f32[2]{0:T(128)S(1)} %copy-done.6), custom_call_target="tpu_custom_call" | custom-call | tf_op jit(solution)/shard_map/weld/pallas_call | solution.py:611
  78.6 1.1 %copy.9 = f32[3,64,16,128]{3,2,1,0:T(8,128)} copy(f32[3,64,16,128]{3,2,1,0:T(8,128)S(1)} %bitcast.6) | data formatting | bytes 3145728
Async XLA Ops:
  0.0 1.4 %copy-start = (f32[3,64,16,128]{3,2,1,0:T(8,128)S(1)}, f32[3,64,16,128]{3,2,1,0:T(8,128)}, u32[]{:S(2)}) copy-start(f32[3,64,16,128]{3,2,1,0:T(8,128)} %param.12) | copy-start | bytes 4718596
  1.4 1.1 %copy-start.1 = (f32[1536,128]{1,0:T(8,128)S(1)}, f32[1536,128]{1,0:T(8,128)}, u32[]{:S(2)}) copy-start(f32[1536,128]{1,0:T(8,128)} %rows_hbm.1) | copy-start | bytes 2359300
  2.5 1.0 %copy-start.2 = (f32[64,16,128]{2,1,0:T(8,128)S(1)}, f32[64,16,128]{2,1,0:T(8,128)}, u32[]{:S(2)}) copy-start(f32[64,16,128]{2,1,0:T(8,128)} %param.10) | copy-start | bytes 1572868
  3.6 1.0 %copy-start.3 = (s32[64,16,128]{2,1,0:T(8,128)S(1)}, s32[64,16,128]{2,1,0:T(8,128)}, u32[]{:S(2)}) copy-start(s32[64,16,128]{2,1,0:T(8,128)} %param.11) | copy-start | bytes 1572868
  4.6 0.7 copy-start.4
  5.3 0.7 copy-start.5
  6.0 0.7 copy-start.6

commit v4 on v3

--- a/solution.py
+++ b/solution.py
@@ -78,8 +78,8 @@
     owner_hbm, element_hbm, rows_hbm, modulus_hbm, birth_hbm, start_hbm, bounds_ref,
     out_ref,
     owner_ref, element_ref, rows_ref, modulus_ref, birth_ref, start_ref, in_sem,
-    split_ref, place_ref, send_rows, send_ids, got_rows, got_ids, total,
-    ids_send_sem, ids_recv_sem, rows_send_sem, rows_recv_sem,
+    split_ref, place_ref, send_rows, send_ids, column_ids, got_rows, got_ids, total,
+    ready_sem, column_send_sem, column_recv_sem, ids_send_sem, ids_recv_sem, rows_send_sem, rows_recv_sem,
     fields, stress, inverse, forces, born, steps, summed, differed, sliced,
     along_matrix, turning,
     packed, packed_stress, got_ends, got_stress_ends, ends, ends_summed, ends_differed, ends_added,
@@ -104,19 +104,28 @@
     for load in loads:
         load.start()
 
-    def there(step):
-        return lax.rem(gx + step // ny, nx), lax.rem(gy + lax.rem(step, ny), ny)
-
-    def number(device):
-        return device[0] * ny + device[1]
+    def in_column(turn):
+        return lax.rem(gx + turn, nx), gy
+
+    def in_line(turn):
+        return gx, lax.rem(gy + turn, ny)
 
     barrier = pltpu.get_barrier_semaphore()
 
-    def greet(step, carry):
-        pl.semaphore_signal(barrier, inc=1, device_id=there(step), device_id_type=MESH)
-        return carry
-
-    lax.fori_loop(1, tiles, greet, 0)
+    def greet_line(turn, carry):
+        pl.semaphore_signal(barrier, inc=1, device_id=in_line(turn), device_id_type=MESH)
+        return carry
+
+    def greet_column(turn, carry):
+        pl.semaphore_signal(barrier, inc=1, device_id=in_column(turn), device_id_type=MESH)
+        return carry
+
+    def tell_column(turn, carry):
+        pl.semaphore_signal(ready_sem, inc=1, device_id=in_column(turn), device_id_type=MESH)
+        return carry
+
+    lax.fori_loop(1, ny, greet_line, 0)
+    lax.fori_loop(1, nx, greet_column, 0)
 
     has = {-1: (gx > 0, gy > 0), 1: (gx < nx - 1, gy < ny - 1)}
 
@@ -154,6 +163,9 @@
     slot = jnp.concatenate(slots, axis=1).astype(jnp.int32)
     place_ref[...] = owner * CAP + slot
 
+    pl.semaphore_wait(barrier, nx + ny - 2)
+    lax.fori_loop(1, nx, tell_column, 0)
+
     weighed = jnp.concatenate(
         [
             (member * (element // 32).astype(F32)).astype(BF16),
@@ -163,26 +175,35 @@
     )
     slot_of = onehot(iota((CY, count), 0) == slot)
     both = lax.dot_general(weighed, slot_of, (((1,), (1,)), ((), ())), preferred_element_type=F32)
-    send_ids[...] = (32.0 * both[:tiles] + both[tiles:]).reshape(tiles, 1, CY)
+    send_ids[...] = (32.0 * both[:tiles] + both[tiles:]).reshape(nx, ny, 1, CY)
 
     loads[2].wait()
     high, low = halves(rows_ref[...])
     split_ref[:, :CY] = high
     split_ref[:, CY:] = low
 
-    pl.semaphore_wait(barrier, tiles - 1)
-
-    def send_id(step, carry):
-        to = there(step)
+    pl.semaphore_wait(ready_sem, nx - 1)
+
+    def send_ids_down(turn, carry):
+        to = in_column(turn)
         pltpu.make_async_remote_copy(
-            src_ref=send_ids.at[number(to)], dst_ref=got_ids.at[step],
+            src_ref=send_ids.at[to[0]], dst_ref=column_ids.at[turn],
+            send_sem=column_send_sem, recv_sem=column_recv_sem,
+            device_id=to, device_id_type=MESH,
+        ).start()
+        return carry
+
+    lax.fori_loop(1, nx, send_ids_down, 0)
+    column_ids[0] = send_ids[gx]
+
+    def send_ids_along(turn, carry):
+        to = in_line(turn)
+        pltpu.make_async_remote_copy(
+            src_ref=column_ids.at[:, to[1]], dst_ref=got_ids.at[:, turn],
             send_sem=ids_send_sem, recv_sem=ids_recv_sem,
             device_id=to, device_id_type=MESH,
         ).start()
         return carry
-
-    lax.fori_loop(1, tiles, send_id, 0)
-    got_ids[0] = send_ids[number((gx, gy))]
 
     def pack_rows(turn, carry):
         tile_x = lax.rem(gx + turn, nx)
@@ -209,8 +230,13 @@
 
         return carry
 
-    lax.fori_loop(0, nx, pack_rows, 0)
-    got_rows[0] = send_rows[number((gx, gy))]
+    lax.fori_loop(0, 2, pack_rows, 0)
+    from_column = pl.ds(1, nx - 1)
+    pltpu.make_async_copy(column_ids.at[from_column], column_ids.at[from_column], column_recv_sem).wait()
+    lax.fori_loop(1, ny, send_ids_along, 0)
+    got_ids[:, 0] = column_ids[:, gy]
+    lax.fori_loop(2, nx, pack_rows, 0)
+    got_rows[0] = send_rows[gx * ny + gy]
 
     zeros = jnp.zeros((ROWS, CY), F32)
     for hand, slab_at, group_at in ((-1, 0, 0), (1, CX + 1, 3)):
@@ -481,7 +507,8 @@
     lax.fori_loop(0, CX, first_rest, 0, unroll=2)
 
     others = pl.ds(1, tiles - 1)
-    pltpu.make_async_copy(got_ids.at[others], got_ids.at[others], ids_recv_sem).wait()
+    from_line = pl.ds(1, ny - 1)
+    pltpu.make_async_copy(got_ids.at[:, from_line], got_ids.at[:, from_line], ids_recv_sem).wait()
     spread = onehot(iota((CY, group), 0) == lax.rem(iota((CY, group), 1), CAP))
     own_lane = iota((ny, group), 0) == iota((ny, group), 1) // CAP
     total[...] = jnp.zeros_like(total)
@@ -497,7 +524,7 @@
             part = got_rows.at[pl.ds(turn * ny, ny)]
             pltpu.make_async_copy(part, part, rows_recv_sem.at[turn]).wait()
 
-        ids = got_ids[pl.ds(turn * ny, ny)].reshape(ny, CY)
+        ids = got_ids[turn].reshape(ny, CY)
         ids_high = jnp.floor(ids * (1.0 / 32.0))
         ids_low = ids - 32.0 * ids_high
         wide = 32.0 * product(ids_high.astype(BF16), spread) + product(ids_low.astype(BF16), spread)
@@ -596,7 +623,8 @@
 
             lax.fori_loop(0, CX // 2, last, 0)
 
-    pltpu.make_async_copy(send_ids.at[others], send_ids.at[others], ids_send_sem).wait()
+    pltpu.make_async_copy(column_ids.at[from_column], column_ids.at[from_column], column_send_sem).wait()
+    pltpu.make_async_copy(got_ids.at[:, from_line], got_ids.at[:, from_line], ids_send_sem).wait()
     pltpu.make_async_copy(send_rows.at[others], send_rows.at[others], rows_send_sem).wait()
     over(stress_faces + stress_sides, finish)
     for sweep in range(SWEEPS):
@@ -624,11 +652,13 @@
             vmem((count, 2 * CY), BF16),
             vmem((1, count), jnp.int32),
             vmem((tiles, CAP, CY), F32),
-            vmem((tiles, 1, CY), F32),
+            vmem((nx, ny, 1, CY), F32),
+            vmem((nx, ny, 1, CY), F32),
             vmem((tiles, CAP, CY), F32),
-            vmem((tiles, 1, CY), F32),
+            vmem((nx, ny, 1, CY), F32),
             vmem((CELLS, 2 * CY), F32),
-            dma, dma, dma, dma((nx,)),
+            pltpu.SemaphoreType.REGULAR,
+            dma, dma, dma, dma, dma, dma((nx,)),
             vmem((SWEEPS, 3, SLABS) + SLAB, F32),
             vmem((SLABS,) + SLAB, F32),
             vmem((CX,) + SLAB, F32),
@@ -652,7 +682,7 @@
             dma((2,)), dma((2,)), dma((2,)), dma((2,)),
         ],
         compiler_params=pltpu.CompilerParams(
-            collective_id=0, has_side_effects=True, vmem_limit_bytes=48 * 1024 * 1024
+            collective_id=0, has_side_effects=True, vmem_limit_bytes=60 * 1024 * 1024
         ),
         name="weld",
     )(

time: 80.4 us -> 73.7 us (0.917)
  local copies, waits for them, and re-layouts: 7.8 us -> 2.65 us
  Pallas kernels: 71.9 us -> 70.6 us
    unnamed x15 -> x1, local copies, waits for them, and re-layouts: 7.8 us -> 2.65 us
    pallas_call x1, Pallas kernels: 71.9 us -> 70.6 us  [local(): pl.pallas_call(functools.partial(kernel, nx, ny), out_shape=jax.ShapeDtyp...]
where the time goes in v4:
time: 73.7 us; the launch traced here: 73.3 us
  Pallas kernels  70.6 us (96%)
  local copies, waits for them, and re-layouts  2.65 us (4%)
    pallas_call x1, Pallas kernels, local(): pl.pallas_call(functools.partial(kernel, nx, ny), out_shape=jax.ShapeDtyp...  70.6 us
    unnamed x1, local copies, waits for them, and re-layouts  2.65 us

profile of v4, /device:TPU:31, one launch (start us, length us, event | category | flops | bytes accessed | tf_op | source)
XLA Modules:
  0.0 73.3 jit_solution(17235310309515105298)
XLA Ops:
  0.0 70.6 %weld.1 = f32[3,1024,128]{2,1,0:T(8,128)} custom-call(s32[1,1536]{1,0:T(1,128)} %bitcast.10, s32[1,1536]{1,0:T(1,128)} %bitcast.11, f32[1536,128]{1,0:T(8,128)} %rows_hbm.1, f32[1024,128]{1,0:T(8,128)} %bitcast.8, s32[1024,128]{1,0:T(8,128)} %bitcast.9, f32[3,1024,128]{2,1,0:T(8,128)} %bitcast.7, f32[2]{0:T(128)} %bounds_ref.1), custom_call_target="tpu_custom_call" | custom-call | tf_op jit(solution)/shard_map/weld/pallas_call | solution.py:639
  70.6 2.7 %copy.9 = f32[3,64,16,128]{3,2,1,0:T(8,128)} copy(f32[3,64,16,128]{3,2,1,0:T(8,128)} %bitcast.6) | data formatting | bytes 3145728

commit v5 on v4

--- a/solution.py
+++ b/solution.py
@@ -9,6 +9,8 @@
 
 SWEEPS = 4
 CAP = 24
+FIRST = 2
+SECOND = 4
 NZ = 64
 CX = 16
 CY = 128
@@ -166,6 +168,40 @@
     pl.semaphore_wait(barrier, nx + ny - 2)
     lax.fori_loop(1, nx, tell_column, 0)
 
+    loads[2].wait()
+    high, low = halves(rows_ref[...])
+    split_ref[:, :CY] = high
+    split_ref[:, CY:] = low
+
+    pl.semaphore_wait(ready_sem, nx - 1)
+
+    def pack_rows(turn, carry):
+        tile_x = lax.rem(gx + turn, nx)
+        wanted = tile_x * group + iota((group, count), 0)
+        picked = product(onehot(wanted == place_ref[...]), split_ref[...])
+        send_rows[pl.ds(tile_x * ny, ny)] = (picked[:, :CY] + picked[:, CY:]).reshape(ny, CAP, CY)
+
+        def send(turn_y, carry):
+            tile_y = lax.rem(gy + turn_y, ny)
+            pltpu.make_async_remote_copy(
+                src_ref=send_rows.at[tile_x * ny + tile_y], dst_ref=got_rows.at[turn * ny + turn_y],
+                send_sem=rows_send_sem, recv_sem=rows_recv_sem.at[turn],
+                device_id=(tile_x, tile_y), device_id_type=MESH,
+            ).start()
+            return carry
+
+        @pl.when(turn == 0)
+        def _():
+            lax.fori_loop(1, ny, send, 0)
+
+        @pl.when(turn > 0)
+        def _():
+            lax.fori_loop(0, ny, send, 0)
+
+        return carry
+
+    lax.fori_loop(0, FIRST, pack_rows, 0)
+
     weighed = jnp.concatenate(
         [
             (member * (element // 32).astype(F32)).astype(BF16),
@@ -177,13 +213,6 @@
     both = lax.dot_general(weighed, slot_of, (((1,), (1,)), ((), ())), preferred_element_type=F32)
     send_ids[...] = (32.0 * both[:tiles] + both[tiles:]).reshape(nx, ny, 1, CY)
 
-    loads[2].wait()
-    high, low = halves(rows_ref[...])
-    split_ref[:, :CY] = high
-    split_ref[:, CY:] = low
-
-    pl.semaphore_wait(ready_sem, nx - 1)
-
     def send_ids_down(turn, carry):
         to = in_column(turn)
         pltpu.make_async_remote_copy(
@@ -204,39 +233,6 @@
             device_id=to, device_id_type=MESH,
         ).start()
         return carry
-
-    def pack_rows(turn, carry):
-        tile_x = lax.rem(gx + turn, nx)
-        wanted = tile_x * group + iota((group, count), 0)
-        picked = product(onehot(wanted == place_ref[...]), split_ref[...])
-        send_rows[pl.ds(tile_x * ny, ny)] = (picked[:, :CY] + picked[:, CY:]).reshape(ny, CAP, CY)
-
-        def send(turn_y, carry):
-            tile_y = lax.rem(gy + turn_y, ny)
-            pltpu.make_async_remote_copy(
-                src_ref=send_rows.at[tile_x * ny + tile_y], dst_ref=got_rows.at[turn * ny + turn_y],
-                send_sem=rows_send_sem, recv_sem=rows_recv_sem.at[turn],
-                device_id=(tile_x, tile_y), device_id_type=MESH,
-            ).start()
-            return carry
-
-        @pl.when(turn == 0)
-        def _():
-            lax.fori_loop(1, ny, send, 0)
-
-        @pl.when(turn > 0)
-        def _():
-            lax.fori_loop(0, ny, send, 0)
-
-        return carry
-
-    lax.fori_loop(0, 2, pack_rows, 0)
-    from_column = pl.ds(1, nx - 1)
-    pltpu.make_async_copy(column_ids.at[from_column], column_ids.at[from_column], column_recv_sem).wait()
-    lax.fori_loop(1, ny, send_ids_along, 0)
-    got_ids[:, 0] = column_ids[:, gy]
-    lax.fori_loop(2, nx, pack_rows, 0)
-    got_rows[0] = send_rows[gx * ny + gy]
 
     zeros = jnp.zeros((ROWS, CY), F32)
     for hand, slab_at, group_at in ((-1, 0, 0), (1, CX + 1, 3)):
@@ -472,8 +468,15 @@
         return carry
 
     lax.fori_loop(0, CX // 2, begin, 0)
+    over(edges(0), start)
     over(faces(0), start)
-    over(edges(0), start)
+    lax.fori_loop(FIRST, SECOND, pack_rows, 0)
+    from_column = pl.ds(1, nx - 1)
+    pltpu.make_async_copy(column_ids.at[from_column], column_ids.at[from_column], column_recv_sem).wait()
+    lax.fori_loop(1, ny, send_ids_along, 0)
+    got_ids[:, 0] = column_ids[:, gy]
+    lax.fori_loop(SECOND, nx, pack_rows, 0)
+    got_rows[0] = send_rows[gx * ny + gy]
 
     loads[4].wait()
     loads[5].wait()
@@ -524,17 +527,21 @@
             part = got_rows.at[pl.ds(turn * ny, ny)]
             pltpu.make_async_copy(part, part, rows_recv_sem.at[turn]).wait()
 
-        ids = got_ids[turn].reshape(ny, CY)
-        ids_high = jnp.floor(ids * (1.0 / 32.0))
-        ids_low = ids - 32.0 * ids_high
-        wide = 32.0 * product(ids_high.astype(BF16), spread) + product(ids_low.astype(BF16), spread)
-        flat = jnp.sum(jnp.where(own_lane, wide, 0.0), axis=0, keepdims=True).astype(jnp.int32) - 1
-        place = onehot(iota((CELLS, group), 0) == flat)
-        high, low = halves(got_rows[pl.ds(turn * ny, ny)].reshape(group, CY))
-        total[...] += product(place, jnp.concatenate([high, low], axis=1))
-        return carry
-
-    lax.fori_loop(0, nx, collect, 0)
+        part = got_rows.at[pl.ds((turn + 1) * ny, ny)]
+        pltpu.make_async_copy(part, part, rows_recv_sem.at[turn + 1]).wait()
+        places = []
+        for at in range(2):
+            ids = got_ids[turn + at].reshape(ny, CY)
+            ids_high = jnp.floor(ids * (1.0 / 32.0))
+            ids_low = ids - 32.0 * ids_high
+            wide = 32.0 * product(ids_high.astype(BF16), spread) + product(ids_low.astype(BF16), spread)
+            flat = jnp.sum(jnp.where(own_lane, wide, 0.0), axis=0, keepdims=True).astype(jnp.int32) - 1
+            places.append(onehot(iota((CELLS, group), 0) == flat))
+        high, low = halves(got_rows[pl.ds(turn * ny, 2 * ny)].reshape(2 * group, CY))
+        total[...] += product(jnp.concatenate(places, axis=1), jnp.concatenate([high, low], axis=1))
+        return carry
+
+    lax.fori_loop(0, nx // 2, lambda pair, carry: collect(2 * pair, carry), 0)
 
     def strain(i, carry):
         at = pl.ds(2 * i * NZ, 2 * NZ)
@@ -639,7 +646,7 @@
     moved = pl.pallas_call(
         functools.partial(kernel, nx, ny),
         out_shape=jax.ShapeDtypeStruct((3, CELLS, CY), F32),
-        in_specs=[pl.BlockSpec(memory_space=pl.ANY)] * 6 + [pl.BlockSpec(memory_space=pltpu.SMEM)],
+        in_specs=[pl.BlockSpec(memory_space=pltpu.HBM)] * 6 + [pl.BlockSpec(memory_space=pltpu.SMEM)],
         out_specs=pl.BlockSpec(memory_space=pltpu.VMEM),
         scratch_shapes=[
             vmem((1, count), jnp.int32),

time: 73.7 us -> 69.7 us (0.946)
  Pallas kernels: 70.6 us -> 66.6 us
    pallas_call x1, Pallas kernels: 70.6 us -> 66.6 us  [local(): pl.pallas_call(functools.partial(kernel, nx, ny), out_shape=jax.ShapeDtyp...]
where the time goes in v5:
time: 69.7 us; the launch traced here: 69.3 us
  Pallas kernels  66.6 us (96%)
  local copies, waits for them, and re-layouts  2.65 us (4%)
    pallas_call x1, Pallas kernels, local(): pl.pallas_call(functools.partial(kernel, nx, ny), out_shape=jax.ShapeDtyp...  66.6 us
    unnamed x1, local copies, waits for them, and re-layouts  2.65 us

profile of v5, /device:TPU:31, one launch (start us, length us, event | category | flops | bytes accessed | tf_op | source)
XLA Modules:
  0.0 69.3 jit_solution(1444698601718627182)
XLA Ops:
  0.0 66.6 %weld.1 = f32[3,1024,128]{2,1,0:T(8,128)} custom-call(s32[1,1536]{1,0:T(1,128)} %bitcast.10, s32[1,1536]{1,0:T(1,128)} %bitcast.11, f32[1536,128]{1,0:T(8,128)} %rows_hbm.1, f32[1024,128]{1,0:T(8,128)} %bitcast.8, s32[1024,128]{1,0:T(8,128)} %bitcast.9, f32[3,1024,128]{2,1,0:T(8,128)} %bitcast.7, f32[2]{0:T(128)} %bounds_ref.1), custom_call_target="tpu_custom_call" | custom-call | tf_op jit(solution)/shard_map/weld/pallas_call | solution.py:646
  66.6 2.7 %copy.9 = f32[3,64,16,128]{3,2,1,0:T(8,128)} copy(f32[3,64,16,128]{3,2,1,0:T(8,128)} %bitcast.6) | data formatting | bytes 3145728

commit v6 on v5

--- a/solution.py
+++ b/solution.py
@@ -9,6 +9,7 @@
 
 SWEEPS = 4
 CAP = 24
+TOGETHER = 4
 FIRST = 2
 SECOND = 4
 NZ = 64
@@ -84,7 +85,7 @@
     ready_sem, column_send_sem, column_recv_sem, ids_send_sem, ids_recv_sem, rows_send_sem, rows_recv_sem,
     fields, stress, inverse, forces, born, steps, summed, differed, sliced,
     along_matrix, turning,
-    packed, packed_stress, got_ends, got_stress_ends, ends, ends_summed, ends_differed, ends_added,
+    packed, corner_rows, packed_stress, got_ends, got_stress_ends, ends, ends_summed, ends_differed, ends_added,
     face_send, face_recv, side_send, side_recv, corner_send, corner_recv,
     stress_face_send, stress_face_recv, stress_side_send, stress_side_recv,
 ):
@@ -235,6 +236,7 @@
         return carry
 
     zeros = jnp.zeros((ROWS, CY), F32)
+    corner_rows[...] = jnp.zeros_like(corner_rows)
     for hand, slab_at, group_at in ((-1, 0, 0), (1, CX + 1, 3)):
 
         @pl.when(jnp.logical_not(has[hand][0]))
@@ -282,6 +284,14 @@
             [jnp.where(first_half, even, turn_halves(odd)), jnp.where(first_half, turn_halves(even), odd)], axis=0
         ).T
 
+    def over_pairs(body):
+        def some(i, carry):
+            for at in range(TOGETHER):
+                body(TOGETHER * i + at, 3 * at)
+            return carry
+
+        lax.fori_loop(0, CX // 2 // TOGETHER, some, 0)
+
     def rows_of(x, part):
         return pl.ds(part * ROWS * CX + x, ROWS, stride=CX)
 
@@ -314,7 +324,7 @@
     def corner(sweep, a, b):
         mine, theirs = (0, 3) if a < 0 else (1, 0)
         return pltpu.make_async_remote_copy(
-            src_ref=packed.at[sweep, :, mine], dst_ref=got_ends.at[sweep, (1 - b) // 2, :, theirs],
+            src_ref=corner_rows.at[sweep, :, mine], dst_ref=got_ends.at[sweep, (1 - b) // 2, :, theirs],
             send_sem=corner_send.at[sweep, a + 1 + (b + 1) // 2], recv_sem=corner_recv.at[sweep, 1 - a + (1 - b) // 2],
             device_id=(gx + a, gy + b), device_id_type=MESH,
         )
@@ -339,10 +349,11 @@
     def faces(sweep):
         return [((a, 0), lambda a=a: face(sweep, a)) for a in pair_of]
 
-    def edges(sweep):
-        return [((0, b), lambda b=b: side(sweep, b)) for b in pair_of] + [
-            ((a, b), lambda a=a, b=b: corner(sweep, a, b)) for a in pair_of for b in pair_of
-        ]
+    def sides(sweep):
+        return [((0, b), lambda b=b: side(sweep, b)) for b in pair_of]
+
+    def corners(sweep):
+        return [((a, b), lambda a=a, b=b: corner(sweep, a, b)) for a in pair_of for b in pair_of]
 
     stress_faces = [((a, 0), lambda a=a: stress_face(a)) for a in pair_of]
     stress_sides = [((0, b), lambda b=b: stress_side(b)) for b in pair_of]
@@ -458,18 +469,23 @@
     def store_ends(slab, x, ref):
         ref[x // ROWS, pl.ds(lax.rem(x, ROWS), 1), :] = end_row(slab)
 
-    def begin(i, carry):
+    def keep_corners(sweep, which):
+        row = pl.ds((ROWS - 1) * which, 1)
         for c in range(3):
-            for odd, slab in enumerate(slabs_of(take(start_ref.at[c], i), c)):
+            corner_rows[sweep, c, which, row, :] = packed[sweep, c, which, row, :]
+
+    def begin(i, room):
+        for c in range(3):
+            for odd, slab in enumerate(slabs_of(take(start_ref.at[c], i), room + c)):
                 x = 2 * i + odd
                 fields[0, c, x + 1] = slab
                 slice_up(slab, c * SLABS + x + 1)
                 store_ends(slab, x, packed.at[0, c])
-        return carry
-
-    lax.fori_loop(0, CX // 2, begin, 0)
-    over(edges(0), start)
-    over(faces(0), start)
+
+    over_pairs(begin)
+    for which in range(2):
+        keep_corners(0, which)
+    over(corners(0) + sides(0) + faces(0), start)
     lax.fori_loop(FIRST, SECOND, pack_rows, 0)
     from_column = pl.ds(1, nx - 1)
     pltpu.make_async_copy(column_ids.at[from_column], column_ids.at[from_column], column_recv_sem).wait()
@@ -481,16 +497,15 @@
     loads[4].wait()
     loads[5].wait()
 
-    def material(i, carry):
-        for odd, modulus in enumerate(slabs_of(take(modulus_ref, i), 0)):
+    def material(i, room):
+        for odd, modulus in enumerate(slabs_of(take(modulus_ref, i), room)):
             x = 2 * i + odd
             stress[x + 1] = modulus
             inverse[x] = 1.0 / (DIAGONAL_WEIGHT * modulus)
-        for odd, birth in enumerate(slabs_of(take(birth_ref, i).astype(F32), 1)):
+        for odd, birth in enumerate(slabs_of(take(birth_ref, i).astype(F32), room + 1)):
             born[2 * i + odd] = birth
-        return carry
-
-    lax.fori_loop(0, CX // 2, material, 0)
+
+    over_pairs(material)
     along_own(0)
 
     lower = jnp.full((ROWS, CY), bounds_ref[0], F32)
@@ -543,17 +558,16 @@
 
     lax.fori_loop(0, nx // 2, lambda pair, carry: collect(2 * pair, carry), 0)
 
-    def strain(i, carry):
+    def strain(i, room):
         at = pl.ds(2 * i * NZ, 2 * NZ)
-        for odd, slab in enumerate(slabs_of(total[at, :CY] + total[at, CY:], 0)):
+        for odd, slab in enumerate(slabs_of(total[at, :CY] + total[at, CY:], room)):
             x = 2 * i + odd
             slab = stress[x + 1] * slab
             stress[x + 1] = slab
             slice_up(slab, x + 1)
             store_ends(slab, x, packed_stress)
-        return carry
-
-    lax.fori_loop(0, CX // 2, strain, 0)
+
+    over_pairs(strain)
     over(stress_faces, start)
     over(stress_sides, start)
     at = pl.ds(1, CX)
@@ -589,9 +603,11 @@
 
     def ends_first(move, sweep):
         lax.fori_loop(0, 2, lambda i, carry: (move(i * (CX - 1)), carry)[1], 0, unroll=2)
-        over(faces(sweep + 1), start)
+        for which in range(2):
+            keep_corners(sweep + 1, which)
+        over(corners(sweep + 1) + faces(sweep + 1), start)
         lax.fori_loop(1, CX - 1, lambda x, carry: (move(x), carry)[1], 0, unroll=2)
-        over(edges(sweep + 1), start)
+        over(sides(sweep + 1), start)
         along_own(sweep + 1)
 
     ends_first(first_move, 0)
@@ -618,24 +634,23 @@
             ends_first(move, sweep)
         else:
 
-            def last(i, carry, moves=moves):
+            def last(i, room, moves=moves):
                 both = [[moved for _, moved, _ in moves(2 * i + odd)] for odd in range(2)]
                 for c in range(3):
-                    block = pair_of_slabs([both[0][c], both[1][c]], c)
+                    block = pair_of_slabs([both[0][c], both[1][c]], room + c)
                     for odd in range(2):
                         for part in range(NZ // ROWS):
                             first = odd * NZ + part * ROWS
                             out_ref[c, rows_of(2 * i + odd, part), :] = block[first : first + ROWS]
-                return carry
-
-            lax.fori_loop(0, CX // 2, last, 0)
+
+            over_pairs(last)
 
     pltpu.make_async_copy(column_ids.at[from_column], column_ids.at[from_column], column_send_sem).wait()
     pltpu.make_async_copy(got_ids.at[:, from_line], got_ids.at[:, from_line], ids_send_sem).wait()
     pltpu.make_async_copy(send_rows.at[others], send_rows.at[others], rows_send_sem).wait()
     over(stress_faces + stress_sides, finish)
     for sweep in range(SWEEPS):
-        over(edges(sweep) + faces(sweep), finish)
+        over(corners(sweep) + sides(sweep) + faces(sweep), finish)
 
 
 def local(thermal_rows, row_owner, row_element, modulus, birth, start_disp, bounds):
@@ -676,7 +691,8 @@
             vmem((3 * SLABS,) + SLAB, F32),
             vmem((3 * SLABS, NZ, 2 * CY), BF16),
             vmem((2 * CY, 2 * CY), BF16),
-            vmem((6, NZ, CY), F32),
+            vmem((6 * TOGETHER, NZ, CY), F32),
+            vmem((SWEEPS, 3, 2, ROWS, CY), F32),
             vmem((SWEEPS, 3, 2, ROWS, CY), F32),
             vmem((2, ROWS, CY), F32),
             vmem((SWEEPS, 2, 3, 4, ROWS, CY), F32),

time: 69.7 us -> 65 us (0.933)
  Pallas kernels: 66.6 us -> 61.5 us
    pallas_call x1, Pallas kernels: 66.6 us -> 61.5 us  [local(): pl.pallas_call(functools.partial(kernel, nx, ny), out_shape=jax.ShapeDtyp...]
where the time goes in v6:
time: 65 us; the launch traced here: 64.2 us
  Pallas kernels  61.5 us (95%)
  local copies, waits for them, and re-layouts  2.65 us (4%)
    pallas_call x1, Pallas kernels, local(): pl.pallas_call(functools.partial(kernel, nx, ny), out_shape=jax.ShapeDtyp...  61.5 us
    unnamed x1, local copies, waits for them, and re-layouts  2.65 us

profile of v6, /device:TPU:31, one launch (start us, length us, event | category | flops | bytes accessed | tf_op | source)
XLA Modules:
  0.0 64.2 jit_solution(6732588256038250518)
XLA Ops:
  0.0 61.5 %weld.1 = f32[3,1024,128]{2,1,0:T(8,128)} custom-call(s32[1,1536]{1,0:T(1,128)} %bitcast.10, s32[1,1536]{1,0:T(1,128)} %bitcast.11, f32[1536,128]{1,0:T(8,128)} %rows_hbm.1, f32[1024,128]{1,0:T(8,128)} %bitcast.8, s32[1024,128]{1,0:T(8,128)} %bitcast.9, f32[3,1024,128]{2,1,0:T(8,128)} %bitcast.7, f32[2]{0:T(128)} %bounds_ref.1), custom_call_target="tpu_custom_call" | custom-call | tf_op jit(solution)/shard_map/weld/pallas_call | solution.py:661
  61.5 2.7 %copy.9 = f32[3,64,16,128]{3,2,1,0:T(8,128)} copy(f32[3,64,16,128]{3,2,1,0:T(8,128)} %bitcast.6) | data formatting | bytes 3145728

commit v7 on v6

--- a/solution.py
+++ b/solution.py
@@ -9,7 +9,7 @@
 
 SWEEPS = 4
 CAP = 24
-TOGETHER = 4
+TOGETHER = 8
 FIRST = 2
 SECOND = 4
 NZ = 64
@@ -127,7 +127,7 @@
         pl.semaphore_signal(ready_sem, inc=1, device_id=in_column(turn), device_id_type=MESH)
         return carry
 
-    lax.fori_loop(1, ny, greet_line, 0)
+    lax.fori_loop(1, ny, greet_line, 0, unroll=5)
     lax.fori_loop(1, nx, greet_column, 0)
 
     has = {-1: (gx > 0, gy > 0), 1: (gx < nx - 1, gy < ny - 1)}
@@ -193,11 +193,11 @@
 
         @pl.when(turn == 0)
         def _():
-            lax.fori_loop(1, ny, send, 0)
+            lax.fori_loop(1, ny, send, 0, unroll=5)
 
         @pl.when(turn > 0)
         def _():
-            lax.fori_loop(0, ny, send, 0)
+            lax.fori_loop(0, ny, send, 0, unroll=4)
 
         return carry
 
@@ -522,7 +522,7 @@
             steps[c, x] = rest(0, x, c)
         return carry
 
-    lax.fori_loop(0, CX, first_rest, 0, unroll=2)
+    lax.fori_loop(0, CX, first_rest, 0, unroll=4)
 
     others = pl.ds(1, tiles - 1)
     from_line = pl.ds(1, ny - 1)
@@ -567,8 +567,16 @@
             slice_up(slab, x + 1)
             store_ends(slab, x, packed_stress)
 
-    over_pairs(strain)
+    strain(0, 0)
+    strain(CX // 2 - 1, 3)
     over(stress_faces, start)
+
+    def strain_inner(k, carry):
+        for at in range(3):
+            strain(1 + 3 * k + at, 3 * at)
+        return carry
+
+    lax.fori_loop(0, 2, strain_inner, 0)
     over(stress_sides, start)
     at = pl.ds(1, CX)
     differed[at] = product(sliced[at].reshape(CX * NZ, 2 * CY), along_matrix[:, CY:]).reshape((CX,) + SLAB)

time: 65 us -> 64.5 us (level)
  Pallas kernels: 61.5 us -> 60.6 us
    pallas_call x1, Pallas kernels: 61.5 us -> 60.6 us  [local(): pl.pallas_call(functools.partial(kernel, nx, ny), out_shape=jax.ShapeDtyp...]
where the time goes in v7:
time: 64.5 us; the launch traced here: 63.3 us
  Pallas kernels  60.6 us (94%)
  local copies, waits for them, and re-layouts  2.65 us (4%)
    pallas_call x1, Pallas kernels, local(): pl.pallas_call(functools.partial(kernel, nx, ny), out_shape=jax.ShapeDtyp...  60.6 us
    unnamed x1, local copies, waits for them, and re-layouts  2.65 us

profile of v7, /device:TPU:31, one launch (start us, length us, event | category | flops | bytes accessed | tf_op | source)
XLA Modules:
  0.0 63.3 jit_solution(876232306470844094)
XLA Ops:
  0.0 60.6 %weld.1 = f32[3,1024,128]{2,1,0:T(8,128)} custom-call(s32[1,1536]{1,0:T(1,128)} %bitcast.10, s32[1,1536]{1,0:T(1,128)} %bitcast.11, f32[1536,128]{1,0:T(8,128)} %rows_hbm.1, f32[1024,128]{1,0:T(8,128)} %bitcast.8, s32[1024,128]{1,0:T(8,128)} %bitcast.9, f32[3,1024,128]{2,1,0:T(8,128)} %bitcast.7, f32[2]{0:T(128)} %bounds_ref.1), custom_call_target="tpu_custom_call" | custom-call | tf_op jit(solution)/shard_map/weld/pallas_call | solution.py:669
  60.6 2.7 %copy.9 = f32[3,64,16,128]{3,2,1,0:T(8,128)} copy(f32[3,64,16,128]{3,2,1,0:T(8,128)} %bitcast.6) | data formatting | bytes 3145728
